TPU v7x, 32 devices: a whole 2x2x4 slice. The times are simulated.
32 devices in a mesh: wide: 8 (over z, y), narrow: 4 (over x, core).
Axes of the slice: x: 2, y: 2, z: 4, core: 2. Of those that a mesh axis runs over, the one named last changes fastest.
Arguments:
- frames: bfloat16 [128, 8, 5, 32, 32, 3], P(('wide', 'narrow')), may hold values from -11 to 11
- tokens: bfloat16 [50176, 2048], P(('wide', 'narrow')), may hold values from -11 to 11
- stem_cotangent: bfloat16 [262144, 64], P(('wide', 'narrow')), may hold values from -6 to 6
- crop_counts: int32 [64], replicated, may hold values from 1 to 5, 128 in all
- labels: int32 [64], replicated, may hold values from 0 to 173
- stem_weight: bfloat16 [588, 64], P(None, 'wide'), may hold values from -0.25 to 0.25
- stem_gain: bfloat16 [64], P('wide'), may hold values from 0.099609375 to 1.8984375
- stem_shift: bfloat16 [64], P('wide'), may hold values from -2 to 2
- w_squeeze: bfloat16 [2048, 512], P('wide'), may hold values from -0.125 to 0.125
- next_kernel: bfloat16 [9, 512], P(None, 'wide'), may hold values from -2 to 2
- scale_kernel: bfloat16 [9, 512], P(None, 'wide'), may hold values from -2 to 2
- w_expand: bfloat16 [512, 2048], P(None, 'wide'), may hold values from -0.25 to 0.25
- w_reduce: bfloat16 [2048, 512], P('wide'), may hold values from -0.125 to 0.125
- gain_one: bfloat16 [512], P('wide'), may hold values from 0.099609375 to 1.8984375
- shift_one: bfloat16 [512], P('wide'), may hold values from -2 to 2
- w_spatial: bfloat16 [9, 512, 512], P(None, 'wide'), may hold values from -0.09375 to 0.09375
- gain_two: bfloat16 [512], P('wide'), may hold values from 0.099609375 to 1.8984375
- shift_two: bfloat16 [512], P('wide'), may hold values from -2 to 2
- w_restore: bfloat16 [512, 2048], P('wide'), may hold values from -0.25 to 0.25
- gain_three: bfloat16 [2048], P('wide'), may hold values from 0.099609375 to 1.8984375
- shift_three: bfloat16 [2048], P('wide'), may hold values from -2 to 2
- w_class: bfloat16 [2048, 174], P('wide'), may hold values from -0.5 to 0.5
- class_bias: bfloat16 [174], replicated, may hold values from -3 to 3
Outputs:
- activations: bfloat16 [50176, 2048], P(('wide', 'narrow'))
- stem_features: bfloat16 [262144, 64], P(('wide', 'narrow'))
- tokens_grad: bfloat16 [50176, 2048], P(('wide', 'narrow'))
- stem_weight_grad: float32 [588, 64], P(None, 'wide')
- stem_gain_grad: float32 [64], P('wide')
- stem_shift_grad: float32 [64], P('wide')
- squeeze_grad: float32 [2048, 512], P('wide')
- next_kernel_grad: float32 [9, 512], P(None, 'wide')
- scale_kernel_grad: float32 [9, 512], P(None, 'wide')
- expand_grad: float32 [512, 2048], P(None, 'wide')
- reduce_grad: float32 [2048, 512], P('wide')
- gain_one_grad: float32 [512], P('wide')
- shift_one_grad: float32 [512], P('wide')
- spatial_grad: float32 [9, 512, 512], P(None, 'wide')
- gain_two_grad: float32 [512], P('wide')
- shift_two_grad: float32 [512], P('wide')
- restore_grad: float32 [512, 2048], P('wide')
- gain_three_grad: float32 [2048], P('wide')
- shift_three_grad: float32 [2048], P('wide')
- class_grad: float32 [2048, 174], P('wide')
- class_bias_grad: float32 [174], replicated
- loss: float32 [], replicated
Inputs may be any that keep to these rules, and one draw needn't show every extreme that they name: `crop_counts`: the counts sum to 128, and some video has 5 views.
All inputs are finite; a program needn't handle non-finite values.
Results may differ from a plain program's by a relative error of at most 0.015.
Values may be sent and summed in bfloat16 or wider, within the bound.
No kernel may reach another device: no remote copies, remote signals or barrier semaphores. Data moves between devices by JAX's collectives and lax.ppermute only.
A program may use at most 320 MiB of HBM per device.

v0:
```python
import jax
import jax.numpy as jnp
from jax import lax
from jax.sharding import PartitionSpec as P

C = 2048
B = 512
R = 512
CLASSES = 174
SEG = 8
SIDE = 7


epsilon = 1e-05
loss_scale = 1024.0


def product(first_operand, second_operand):
    return jnp.dot(first_operand, second_operand, preferred_element_type=jnp.float32)


def product_left(first_operand, second_operand):
    return lax.dot_general(
        first_operand, second_operand, (((0,), (0,)), ((), ())), preferred_element_type=jnp.float32
    )


def product_right(first_operand, second_operand):
    return lax.dot_general(
        first_operand, second_operand, (((1,), (1,)), ((), ())), preferred_element_type=jnp.float32
    )


def depthwise(feature, kernel):
    extent = feature.shape[2]
    padded = jnp.pad(feature, ((0, 0), (0, 0), (1, 1), (1, 1), (0, 0)))
    accumulated = jnp.zeros_like(feature)
    for offset in range(9):
        accumulated = (
            accumulated
            + padded[:, :, offset // 3 : offset // 3 + extent, offset % 3 : offset % 3 + extent, :]
            * kernel[offset]
        )
    return accumulated


def temporal(squeezed, next_kernel, scale_kernel):
    upcoming = jnp.concatenate([squeezed[:, 1:], jnp.zeros_like(squeezed[:, :1])], axis=1)
    differ = depthwise(upcoming, next_kernel) - squeezed
    return differ + depthwise(differ, scale_kernel) + jnp.mean(differ, axis=(2, 3), keepdims=True)


def columns(feature):
    extent = feature.shape[2]
    padded = jnp.pad(feature, ((0, 0), (0, 0), (1, 1), (1, 1), (0, 0)))
    pieces = [
        padded[:, :, offset // 3 : offset // 3 + extent, offset % 3 : offset % 3 + extent, :]
        for offset in range(9)
    ]
    return jnp.concatenate(pieces, axis=-1).reshape(-1, 9 * feature.shape[-1])


def frame_differ(frames):
    differ = jnp.concatenate(
        [frames[:, :, index + 1] - frames[:, :, index] for index in range(4)], axis=-1
    )
    return differ.reshape((-1,) + differ.shape[2:])


def stem_conv(differ, kernel):
    return lax.conv_general_dilated(
        differ,
        kernel,
        (2, 2),
        ((3, 3), (3, 3)),
        dimension_numbers=("NHWC", "HWIO", "NHWC"),
        preferred_element_type=jnp.float32,
    )


def silu_slope(values):
    sigma = jax.nn.sigmoid(values)
    return sigma * (1.0 + values * (1.0 - sigma))


def norm_forward(values, gain, shift, count):
    sums, squares = lax.psum((jnp.sum(values, 0), jnp.sum(values * values, 0)), ("wide", "narrow"))
    mean = sums / count
    inverse = lax.rsqrt(squares / count - mean * mean + epsilon)
    unit = (values - mean) * inverse
    return (unit * gain + shift, unit, inverse)


def norm_backward(grad, unit, inverse, gain, count):
    shift_grad, gain_grad = lax.psum(
        (jnp.sum(grad, 0), jnp.sum(grad * unit, 0)), ("wide", "narrow")
    )
    value_grad = gain * inverse * (grad - shift_grad / count - unit * gain_grad / count)
    return (value_grad, gain_grad, shift_grad)


def own_slice(values, width):
    return lax.dynamic_slice_in_dim(values, lax.axis_index("wide") * width, width)


def shards(
    frames,
    tokens,
    stem_cotangent,
    crop_counts,
    labels,
    stem_weight,
    stem_gain,
    stem_shift,
    w_squeeze,
    next_kernel,
    scale_kernel,
    w_expand,
    w_reduce,
    gain_one,
    shift_one,
    w_spatial,
    gain_two,
    shift_two,
    w_restore,
    gain_three,
    shift_three,
    w_class,
    class_bias,
):
    f32 = jnp.float32
    bf16 = jnp.bfloat16
    view_count = frames.shape[0]
    row_count = tokens.shape[0]
    devices = lax.axis_size(("wide", "narrow"))
    count = float(row_count * devices)
    (
        full_stem,
        full_stem_gain,
        full_stem_shift,
        full_squeeze,
        full_next,
        full_scale,
        full_expand,
        full_reduce,
        full_gain_one,
        full_shift_one,
        full_spatial,
        full_gain_two,
        full_shift_two,
        full_restore,
        full_gain_three,
        full_shift_three,
        full_class,
    ) = (
        lax.all_gather(stem_weight, "wide", axis=1, tiled=True),
        lax.all_gather(stem_gain, "wide", axis=0, tiled=True),
        lax.all_gather(stem_shift, "wide", axis=0, tiled=True),
        lax.all_gather(w_squeeze, "wide", axis=0, tiled=True),
        lax.all_gather(next_kernel, "wide", axis=1, tiled=True),
        lax.all_gather(scale_kernel, "wide", axis=1, tiled=True),
        lax.all_gather(w_expand, "wide", axis=1, tiled=True),
        lax.all_gather(w_reduce, "wide", axis=0, tiled=True),
        lax.all_gather(gain_one, "wide", axis=0, tiled=True),
        lax.all_gather(shift_one, "wide", axis=0, tiled=True),
        lax.all_gather(w_spatial, "wide", axis=1, tiled=True),
        lax.all_gather(gain_two, "wide", axis=0, tiled=True),
        lax.all_gather(shift_two, "wide", axis=0, tiled=True),
        lax.all_gather(w_restore, "wide", axis=0, tiled=True),
        lax.all_gather(gain_three, "wide", axis=0, tiled=True),
        lax.all_gather(shift_three, "wide", axis=0, tiled=True),
        lax.all_gather(w_class, "wide", axis=0, tiled=True),
    )
    differ_low = frame_differ(frames.astype(f32)).astype(bf16)
    stem_width_all = full_stem.shape[1]
    stem_kernel = full_stem.reshape(7, 7, differ_low.shape[-1], stem_width_all)
    stem_pre = stem_conv(differ_low, stem_kernel).reshape(-1, stem_width_all)
    stem_count = float(stem_pre.shape[0] * devices)
    stem_norm, stem_unit, stem_inverse = norm_forward(
        stem_pre, full_stem_gain.astype(f32), full_stem_shift.astype(f32), stem_count
    )
    stem_out = jax.nn.silu(stem_norm)
    squeezed = product(tokens, full_squeeze)

    def mixing(squeezed_values, next_values, scale_values):
        return temporal(
            squeezed_values.reshape(view_count, SEG, SIDE, SIDE, R), next_values, scale_values
        ).reshape(row_count, R)

    mixed, mixing_back = jax.vjp(mixing, squeezed, full_next.astype(f32), full_scale.astype(f32))
    mixed_low = mixed.astype(bf16)
    gate = jax.nn.sigmoid(product(mixed_low, full_expand))
    token_values = tokens.astype(f32)
    gated = token_values + token_values * gate
    gated_low = gated.astype(bf16)
    pre_one = product(gated_low, full_reduce)
    norm_one, unit_one, inverse_one = norm_forward(
        pre_one, full_gain_one.astype(f32), full_shift_one.astype(f32), count
    )
    hidden_one = jax.nn.silu(norm_one).astype(bf16)
    spread_cols = columns(hidden_one.reshape(view_count, SEG, SIDE, SIDE, B))
    pre_two = product(spread_cols, full_spatial.reshape(9 * B, B))
    norm_two, unit_two, inverse_two = norm_forward(
        pre_two, full_gain_two.astype(f32), full_shift_two.astype(f32), count
    )
    hidden_two = jax.nn.silu(norm_two).astype(bf16)
    pre_three = product(hidden_two, full_restore)
    norm_three, unit_three, inverse_three = norm_forward(
        pre_three, full_gain_three.astype(f32), full_shift_three.astype(f32), count
    )
    summed = norm_three + gated
    output = jax.nn.silu(summed)
    per_view = SEG * SIDE * SIDE
    pooled = jnp.mean(output.reshape(view_count, per_view, C), 1)
    pooled_low = pooled.astype(bf16)
    view_logits = product(pooled_low, full_class) + class_bias.astype(f32)
    ends = jnp.cumsum(crop_counts)
    starts = ends - crop_counts
    positions = lax.axis_index(("wide", "narrow")) * view_count + jnp.arange(
        view_count, dtype=jnp.int32
    )
    member = (
        (positions[:, None] >= starts[None, :]) & (positions[:, None] < ends[None, :])
    ).astype(f32)
    partial_sums = jnp.dot(
        member.T, view_logits, precision=lax.Precision.HIGHEST, preferred_element_type=f32
    )
    video_sums = lax.psum(partial_sums, ("wide", "narrow"))
    counts_f = crop_counts.astype(f32)
    video_logits = video_sums / counts_f[:, None]
    log_probs = jax.nn.log_softmax(video_logits, axis=-1)
    target = (labels[:, None] == jnp.arange(CLASSES, dtype=jnp.int32)[None, :]).astype(f32)
    loss = jnp.mean(-jnp.sum(target * log_probs, axis=-1))
    video_grad = loss_scale * (jnp.exp(log_probs) - target)
    class_bias_grad = jnp.sum(video_grad, 0)
    view_grad = jnp.dot(
        member,
        video_grad / counts_f[:, None],
        precision=lax.Precision.HIGHEST,
        preferred_element_type=f32,
    )
    view_grad_low = view_grad.astype(bf16)
    (
        back_class,
        back_restore,
        back_gain_three,
        back_spatial,
        back_gain_two,
        back_reduce,
        back_gain_one,
        back_expand,
        back_squeeze,
        back_stem_gain,
    ) = (
        lax.all_gather(w_class, "wide", axis=0, tiled=True),
        lax.all_gather(w_restore, "wide", axis=0, tiled=True),
        lax.all_gather(gain_three, "wide", axis=0, tiled=True),
        lax.all_gather(w_spatial, "wide", axis=1, tiled=True),
        lax.all_gather(gain_two, "wide", axis=0, tiled=True),
        lax.all_gather(w_reduce, "wide", axis=0, tiled=True),
        lax.all_gather(gain_one, "wide", axis=0, tiled=True),
        lax.all_gather(w_expand, "wide", axis=1, tiled=True),
        lax.all_gather(w_squeeze, "wide", axis=0, tiled=True),
        lax.all_gather(stem_gain, "wide", axis=0, tiled=True),
    )
    class_grad = product_left(pooled_low, view_grad_low)
    pooled_grad = product_right(view_grad_low, back_class)
    output_grad = jnp.broadcast_to(
        (pooled_grad / per_view)[:, None, :], (view_count, per_view, C)
    ).reshape(row_count, C)
    summed_grad = output_grad * silu_slope(summed)
    pre_three_grad, gain_three_grad, shift_three_grad = norm_backward(
        summed_grad, unit_three, inverse_three, back_gain_three.astype(f32), count
    )
    low_three = pre_three_grad.astype(bf16)
    restore_grad = product_left(hidden_two, low_three)
    hidden_two_grad = product_right(low_three, back_restore)
    pre_two_grad, gain_two_grad, shift_two_grad = norm_backward(
        hidden_two_grad * silu_slope(norm_two),
        unit_two,
        inverse_two,
        back_gain_two.astype(f32),
        count,
    )
    low_two = pre_two_grad.astype(bf16)
    spatial_grad = product_left(spread_cols, low_two).reshape(9, -1, B)
    cols_grad = product_right(low_two, back_spatial.reshape(9 * B, B))
    spread_back = jax.vjp(columns, jnp.zeros((view_count, SEG, SIDE, SIDE, B), f32))[1]
    hidden_one_grad = spread_back(cols_grad)[0].reshape(row_count, B)
    pre_one_grad, gain_one_grad, shift_one_grad = norm_backward(
        hidden_one_grad * silu_slope(norm_one),
        unit_one,
        inverse_one,
        back_gain_one.astype(f32),
        count,
    )
    low_one = pre_one_grad.astype(bf16)
    reduce_grad = product_left(gated_low, low_one)
    gated_grad = product_right(low_one, back_reduce) + summed_grad
    gate_logit_grad = (gated_grad * token_values * gate * (1.0 - gate)).astype(bf16)
    expand_grad = product_left(mixed_low, gate_logit_grad)
    mixed_grad = product_right(gate_logit_grad, back_expand)
    squeezed_grad, next_grad, scale_grad = mixing_back(mixed_grad)
    low_squeezed = squeezed_grad.astype(bf16)
    squeeze_grad = product_left(tokens, low_squeezed)
    tokens_grad = (gated_grad * (1.0 + gate) + product_right(low_squeezed, back_squeeze)).astype(
        bf16
    )
    stem_norm_grad = stem_cotangent.astype(f32) * silu_slope(stem_norm)
    stem_pre_grad, stem_gain_grad, stem_shift_grad = norm_backward(
        stem_norm_grad, stem_unit, stem_inverse, back_stem_gain.astype(f32), stem_count
    )
    stem_pre_low = stem_pre_grad.astype(bf16).astype(f32)
    differ_values = differ_low.astype(f32)

    def stem_map(kernel_values):
        return stem_conv(differ_values, kernel_values)

    stem_map_back = jax.vjp(stem_map, stem_kernel.astype(f32))[1]
    stem_grad = stem_map_back(
        stem_pre_low.reshape(
            differ_low.shape[0], differ_low.shape[1] // 2, differ_low.shape[2] // 2, stem_width_all
        )
    )[0].reshape(-1, stem_width_all)
    (
        part_stem,
        part_squeeze,
        part_next,
        part_scale,
        part_expand,
        part_reduce,
        part_spatial,
        part_restore,
        part_class,
    ) = (
        lax.psum_scatter(stem_grad, "wide", scatter_dimension=1, tiled=True),
        lax.psum_scatter(squeeze_grad, "wide", scatter_dimension=0, tiled=True),
        lax.psum_scatter(next_grad, "wide", scatter_dimension=1, tiled=True),
        lax.psum_scatter(scale_grad, "wide", scatter_dimension=1, tiled=True),
        lax.psum_scatter(expand_grad, "wide", scatter_dimension=1, tiled=True),
        lax.psum_scatter(reduce_grad, "wide", scatter_dimension=0, tiled=True),
        lax.psum_scatter(spatial_grad, "wide", scatter_dimension=1, tiled=True),
        lax.psum_scatter(restore_grad, "wide", scatter_dimension=0, tiled=True),
        lax.psum_scatter(class_grad, "wide", scatter_dimension=0, tiled=True),
    )
    (
        sum_stem,
        sum_squeeze,
        sum_next,
        sum_scale,
        sum_expand,
        sum_reduce,
        sum_spatial,
        sum_restore,
        sum_class,
    ) = (
        lax.psum(part_stem.astype(jnp.bfloat16), "narrow").astype(jnp.float32),
        lax.psum(part_squeeze.astype(jnp.bfloat16), "narrow").astype(jnp.float32),
        lax.psum(part_next.astype(jnp.bfloat16), "narrow").astype(jnp.float32),
        lax.psum(part_scale.astype(jnp.bfloat16), "narrow").astype(jnp.float32),
        lax.psum(part_expand.astype(jnp.bfloat16), "narrow").astype(jnp.float32),
        lax.psum(part_reduce.astype(jnp.bfloat16), "narrow").astype(jnp.float32),
        lax.psum(part_spatial.astype(jnp.bfloat16), "narrow").astype(jnp.float32),
        lax.psum(part_restore.astype(jnp.bfloat16), "narrow").astype(jnp.float32),
        lax.psum(part_class.astype(jnp.bfloat16), "narrow").astype(jnp.float32),
    )
    stem_width = stem_gain.shape[0]
    inner_width = gain_one.shape[0]
    outer_width = gain_three.shape[0]
    return (
        output.astype(bf16),
        stem_out.astype(bf16),
        tokens_grad,
        sum_stem,
        own_slice(stem_gain_grad, stem_width),
        own_slice(stem_shift_grad, stem_width),
        sum_squeeze,
        sum_next,
        sum_scale,
        sum_expand,
        sum_reduce,
        own_slice(gain_one_grad, inner_width),
        own_slice(shift_one_grad, inner_width),
        sum_spatial,
        own_slice(gain_two_grad, inner_width),
        own_slice(shift_two_grad, inner_width),
        sum_restore,
        own_slice(gain_three_grad, outer_width),
        own_slice(shift_three_grad, outer_width),
        sum_class,
        class_bias_grad,
        loss,
    )


def solution(mesh):
    in_specs = (
        P(("wide", "narrow"), None, None, None, None, None),
        P(("wide", "narrow"), None),
        P(("wide", "narrow"), None),
        P(),
        P(),
        P(None, "wide"),
        P("wide"),
        P("wide"),
        P("wide", None),
        P(None, "wide"),
        P(None, "wide"),
        P(None, "wide"),
        P("wide", None),
        P("wide"),
        P("wide"),
        P(None, "wide", None),
        P("wide"),
        P("wide"),
        P("wide", None),
        P("wide"),
        P("wide"),
        P("wide", None),
        P(),
    )
    out_specs = (
        P(("wide", "narrow"), None),
        P(("wide", "narrow"), None),
        P(("wide", "narrow"), None),
        P(None, "wide"),
        P("wide"),
        P("wide"),
        P("wide", None),
        P(None, "wide"),
        P(None, "wide"),
        P(None, "wide"),
        P("wide", None),
        P("wide"),
        P("wide"),
        P(None, "wide", None),
        P("wide"),
        P("wide"),
        P("wide", None),
        P("wide"),
        P("wide"),
        P("wide", None),
        P(),
        P(),
    )
    return jax.shard_map(shards, mesh=mesh, in_specs=in_specs, out_specs=out_specs, check_vma=False)
```

profile of v0, /device:TPU:0, one launch (start us, length us, event | category | flops | bytes accessed | tf_op | source)
XLA Modules:
  0.0 1568.4 jit_solution(5192477117864547501)
XLA Ops:
  10.6 32.5 %all-gather = bf16[8,64,9]{1,2,0:T(8,128)(2,1)S(1)} all-gather(bf16[1,64,9]{1,2,0:T(8,128)(2,1)} %bitcast.202), channel_id=1, replica_groups=mesh['wide'=8,'narrow'=4] {'wide'}, dimensions={0}, use_global_device_ids=true | all-gather | bytes 10368 | tf_op jit(solution)/shard_map/all_gather | solution.py:160
  43.3 30.7 %all-gather.1 = bf16[8,64,9]{1,2,0:T(8,128)(2,1)S(1)} all-gather(bf16[1,64,9]{1,2,0:T(8,128)(2,1)} %bitcast.203), channel_id=1, replica_groups=mesh['wide'=8,'narrow'=4] {'wide'}, dimensions={0}, use_global_device_ids=true | all-gather | bytes 10368 | tf_op jit(solution)/shard_map/all_gather | solution.py:161
  82.0 22.4 %all-reduce.63 = (bf16[64]{0:T(256)(128)(2,1)S(1)}, bf16[64]{0:T(256)(128)(2,1)S(1)}, bf16[512]{0:T(512)(128)(2,1)S(1)}, bf16[512]{0:T(512)(128)(2,1)S(1)}, bf16...) all-reduce(bf16[64]{0:T(256)(128)(2,1)S(1)} %dynamic-update-slice.5, ...), channel_id=1, replica_groups=mesh['wide'=8,'narrow'=4] {'wide'}, use_global_device_ids=true, to_apply=%add.55 | all-reduce | flops 2176 | bytes 8704
  105.1 16.3 %all-gather.2 = bf16[8,1,256]{2,1,0:T(2,128)(2,1)S(1)} all-gather(bf16[1,1,256]{2,1,0:T(2,128)(2,1)S(1)} %reshape.316), channel_id=1, replica_groups=mesh['wide'=8,'narrow'=4] {'wide'}, dimensions={0}, use_global_device_ids=true | all-gather | bytes 4608 | tf_op jit(solution)/shard_map/all_gather | solution.py:170
  122.1 18.3 %all-gather.3 = bf16[8,1,256]{2,1,0:T(2,128)(2,1)S(1)} all-gather(bf16[1,1,256]{2,1,0:T(2,128)(2,1)S(1)} %reshape.318), channel_id=1, replica_groups=mesh['wide'=8,'narrow'=4] {'wide'}, dimensions={0}, use_global_device_ids=true | all-gather | bytes 4608 | tf_op jit(solution)/shard_map/all_gather | solution.py:171
  140.3 35.6 %all_gather.77 = bf16[2048,174]{0,1:T(8,128)(2,1)} all-gather(bf16[256,174]{0,1:T(8,128)(2,1)} %param.44), channel_id=1, replica_groups=mesh['wide'=8,'narrow'=4] {'wide'}, dimensions={0}, use_global_device_ids=true | all-gather | bytes 801792 | tf_op jit(solution)/shard_map/all_gather | solution.py:172
  190.4 31.4 %all_gather.74 = bf16[588,64]{0,1:T(8,128)(2,1)S(1)} all-gather(bf16[588,8]{0,1:T(8,128)(2,1)S(1)} %copy-done.71), channel_id=1, replica_groups=mesh['wide'=8,'narrow'=4] {'wide'}, dimensions={1}, use_global_device_ids=true | all-gather | bytes 84672 | tf_op jit(solution)/shard_map/all_gather | solution.py:156
  223.0 16.2 %fusion.43 = (f32[64]{0:T(128)}, f32[64]{0:T(128)}, f32[32,16,16,64]{3,0,2,1:T(8,128)S(1)}) fusion(bf16[7,7,12,64]{3,2,1,0:T(8,128)(2,1)S(1)} %reshape.284, bf16[32,32,32,3]{0,3,2,1:T(4,128)(2,1)S(1)} %copy.98, bf16[32,32,32,3]{0,3,2,1:T(4,128)(2,1)} %copy.97, bf16[32,32,32,3]{0,3,2,1:T(4,128)(2,1)} %copy.96, bf16[32,32,32,3]{0,3,2,1:T(4,128)(2,1)S(1)} %copy-done.23), kind=kOutput, calls=%fused_computation.206 | convolution fusion | flops 556990336 | bytes 2959360 | tf_op jit(solution)/shard_map/conv_general_dilated | solution.py:71
  239.2 4.4 copy.100
  245.4 6.2 fusion.58
  260.5 4.0 fusion.52
  266.3 3.9 add_convert_fusion.2
  270.8 9.6 add_divide_fusion.1
  280.5 9.0 fusion.47
  289.5 37.1 %all-reduce.62 = (f32[512]{0:T(512)S(1)}, f32[512]{0:T(512)S(1)}) all-reduce(f32[512]{0:T(512)S(1)} %get-tuple-element.144, f32[512]{0:T(512)S(1)} %get-tuple-element.143), channel_id=1, replica_groups=mesh['wide'=8,'narrow'=4] {'wide','narrow'}, use_global_device_ids=true, to_apply=%region_4.5 | all-reduce | flops 1024 | bytes 8192 | tf_op jit(solution)/shard_map/psum | solution.py:87
  333.0 11.5 pad_slice_fusion.16
  354.6 3.7 concatenate.31
  391.5 13.4 fusion.46
  405.0 42.4 %all-reduce.61 = (f32[512]{0:T(512)S(1)}, f32[512]{0:T(512)S(1)}) all-reduce(f32[512]{0:T(512)S(1)} %get-tuple-element.142, f32[512]{0:T(512)S(1)} %get-tuple-element.141), channel_id=1, replica_groups=mesh['wide'=8,'narrow'=4] {'wide','narrow'}, use_global_device_ids=true, to_apply=%region_8.9 | all-reduce | flops 1024 | bytes 8192 | tf_op jit(solution)/shard_map/psum | solution.py:87
  447.3 11.3 fusion.42
  458.6 38.7 %all-reduce.60 = (f32[2048]{0:T(1024)S(1)}, f32[2048]{0:T(1024)S(1)}) all-reduce(f32[2048]{0:T(1024)S(1)} %get-tuple-element.113, f32[2048]{0:T(1024)S(1)} %get-tuple-element.112), channel_id=1, replica_groups=mesh['wide'=8,'narrow'=4] {'wide','narrow'}, use_global_device_ids=true, to_apply=%region_12.13 | all-reduce | flops 4096 | bytes 32768 | tf_op jit(solution)/shard_map/psum | solution.py:87
  497.3 17.6 %fusion.50 = (bf16[1568,2048]{1,0:T(8,128)(2,1)}, f32[1568,2048]{1,0:T(8,128)}) fusion(f32[1568,2048]{1,0:T(8,128)} %add_divide_fusion.1, bf16[1568,2048]{1,0:T(8,128)(2,1)} %param.24, f32[2048]{0:T(1024)S(1)} %bitcast.144, f32[2048]{0:T(1024)S(1)} %bitcast.140, f32[2048]{0:T(1024)S(1)} %get-tuple-element.246, f32[1568,2048]{1,0:T(8,128)} %get-tuple-element.263, ...), kind=kLoop, calls=%fused_computation.212 | loop fusion | flops 41746432 | bytes 51412992 | tf_op jit(solution)/shard_map/convert_element_type | solution.py:371
  515.0 5.4 reduce_sum.367
  522.1 41.8 %psum.190 = f32[64,174]{1,0:T(8,128)S(1)} all-reduce(f32[64,174]{1,0:T(8,128)S(1)} %fusion.33), channel_id=1, replica_groups=mesh['wide'=8,'narrow'=4] {'wide','narrow'}, use_global_device_ids=true, to_apply=%region_19.20 | all-reduce | flops 11136 | bytes 89088 | tf_op jit(solution)/shard_map/psum | solution.py:228
  567.9 17.5 %fusion.41 = (f32[2048]{0:T(1024)S(1)}, f32[2048]{0:T(1024)S(1)}, f32[1568,2048]{1,0:T(8,128)}) fusion(f32[2048]{0:T(1024)S(1)} %get-tuple-element.246, f32[1568,2048]{1,0:T(8,128)} %get-tuple-element.263, f32[2048]{0:T(1024)S(1)} %get-tuple-element.247, f32[1568,2048]{1,0:T(8,128)} %add_divide_fusion.1, bf16[1568,2048]{1,0:T(8,128)(2,1)} %param.24, ...), kind=kLoop, calls=%fused_computation.204 | loop fusion | flops 61009920 | bytes 45039616 | tf_op jit(solution)/shard_map/reduce_sum | solution.py:96
  585.4 39.1 %all-reduce.59 = (f32[2048]{0:T(1024)S(1)}, f32[2048]{0:T(1024)S(1)}) all-reduce(f32[2048]{0:T(1024)S(1)} %get-tuple-element.111, f32[2048]{0:T(1024)S(1)} %get-tuple-element.110), channel_id=1, replica_groups=mesh['wide'=8,'narrow'=4] {'wide','narrow'}, use_global_device_ids=true, to_apply=%region_25.26 | all-reduce | flops 4096 | bytes 32768 | tf_op jit(solution)/shard_map/psum | solution.py:95
  624.5 10.5 multiply_convert_fusion
  635.1 6.8 fusion.45
  641.9 41.8 %all-reduce.58 = (f32[64]{0:T(128)S(1)}, f32[64]{0:T(128)S(1)}, f32[512]{0:T(512)S(1)}, f32[512]{0:T(512)S(1)}) all-reduce(f32[64]{0:T(128)S(1)} %copy-done.92, f32[64]{0:T(128)S(1)} %copy-done.91, f32[512]{0:T(512)S(1)} %get-tuple-element.140, f32[512]{0:T(512)S(1)} %get-tuple-element.139), channel_id=1, replica_groups=mesh['wide'=8,'narrow'=4] {'wide','narrow'}, use_global_device_ids=true, to_apply=%region_16.17 | all-reduce | flops 1152 | bytes 9216 | tf_op jit(solution)/shard_map/psum | solution.py:87
  683.7 4.9 multiply_convert_fusion.4
  692.3 16.1 %fusion.11 = f32[4,8,7,7,4608]{4,1,3,2,0:T(8,128)} fusion(bf16[4608,512,1,1,1]{1,0,4,3,2:T(8,128)(2,1)} %bitcast.206, bf16[4,8,7,7,512]{4,3,2,1,0:T(8,128)(2,1)} %dot_general.78), kind=kOutput, calls=%fused_computation.134 | convolution fusion | flops 7398752256 | bytes 35225600 | tf_op jit(solution)/shard_map/dot_general | solution.py:29
  708.3 19.5 %fusion.53 = (f32[4,8,7,7,512]{4,1,3,2,0:T(8,128)}, f32[4,8,7,7,512]{4,1,3,2,0:T(8,128)}, f32[4,8,7,7,512]{4,1,3,2,0:T(8,128)}, f32[4,8,7,7,512]{4,1,3,2,0:T(8,1...) fusion(f32[4,8,7,7,4608]{4,1,3,2,0:T(8,128)} %fusion.11), kind=kLoop, calls=%fused_computation.214 | loop fusion | bytes 57802752 | tf_op jit(solution)/shard_map/transpose(jvp())/split | solution.py:60
  727.9 5.3 pad_add_fusion.2
  733.6 5.4 pad_add_fusion.15
  739.0 3.8 copy.103
  742.8 4.7 reshape.290
  747.8 5.4 fusion.44
  756.1 38.8 %all-reduce.57 = (f32[64]{0:T(128)S(1)}, f32[64]{0:T(128)S(1)}, f32[512]{0:T(512)S(1)}, f32[512]{0:T(512)S(1)}) all-reduce(f32[64]{0:T(128)S(1)} %get-tuple-element.132, f32[64]{0:T(128)S(1)} %get-tuple-element.131, f32[512]{0:T(512)S(1)} %get-tuple-element.138, ...), channel_id=1, replica_groups=mesh['wide'=8,'narrow'=4] {'wide','narrow'}, use_global_device_ids=true, to_apply=%region_38.39 | all-reduce | flops 1152 | bytes 9216 | tf_op jit(solution)/shard_map/psum | solution.py:95
  795.5 10.1 fusion.38
  806.3 3.9 multiply_convert_fusion.3
  810.2 17.6 %fusion.2 = (bf16[1568,2048]{1,0:T(8,128)(2,1)}, f32[1568,2048]{1,0:T(8,128)}) fusion(f32[1568,2048]{1,0:T(8,128)} %add_divide_fusion.1, bf16[1568,2048]{1,0:T(8,128)(2,1)} %param.24, f32[1568,2048]{1,0:T(8,128)} %get-tuple-element.180, bf16[1568,512]{1,0:T(8,128)(2,1)} %multiply_convert_fusion.3, bf16[2048,512]{1,0:T(8,128)(2,1)} %all-gather.14.cloned.1.call-done), kind=kOutput, calls=%fused_computation.20 | convolution fusion | flops 3310813184 | bytes 55083008 | tf_op jit(solution)/shard_map/dot_general | solution.py:29
  827.9 6.3 fusion.59
  836.4 24.5 %multiply_reduce_fusion.12 = (f32[512]{0:T(512)S(1)}, f32[512]{0:T(512)S(1)}, f32[512]{0:T(512)S(1)}, f32[512]{0:T(512)S(1)}, f32[512]{0:T(512)S(1)}, /*index=5*...) fusion(f32[4,8,7,7,512]{4,3,2,1,0:T(8,128)} %reshape.291, ...), kind=kLoop, calls=%fused_computation.69 | loop fusion | flops 21655040 | bytes 32212992 | tf_op jit(solution)/shard_map/transpose(jvp())/reduce_sum | solution.py:41
  861.5 9.0 pad_add_fusion.1
  870.6 21.2 %multiply_reduce_fusion.21 = (f32[512]{0:T(512)S(1)}, f32[512]{0:T(512)S(1)}, f32[512]{0:T(512)S(1)}, f32[512]{0:T(512)S(1)}, f32[512]{0:T(512)S(1)}, /*index=5*...) fusion(f32[4,8,7,7,512]{4,3,2,1,0:T(8,128)} %copy-done.2, ...), kind=kLoop, calls=%fused_computation.78 | loop fusion | flops 20868608 | bytes 35006464 | tf_op jit(solution)/shard_map/transpose(jvp())/reduce_sum | solution.py:41
  891.8 10.2 broadcast_multiply_fusion.9
  902.0 10.2 pad_add_fusion
  912.2 7.7 pad_add_fusion.9
  922.3 9.3 convolution_bitcast_fusion
  933.1 8.4 fusion.60
  942.9 13.2 fusion.34
  956.1 19.5 %copy.106 = bf16[4608,1568]{1,0:T(8,128)(2,1)} copy(bf16[4608,1568]{0,1:T(8,128)(2,1)} %bitcast.130) | data formatting | bytes 28901376 | tf_op jit(solution)/shard_map/dot_general | solution.py:23
  975.6 14.4 fusion.9
  992.9 6.0 multiply_convert_fusion.1
  998.9 10.1 fusion.7
  1012.4 8.5 reduce-scatter.14.cloned.1.call-done
  1022.7 90.1 %reduce-scatter.16.cloned.1.call-done = f32[512,256]{1,0:T(8,128)} async-done(((f32[512,2048]{1,0:T(8,128)}), f32[512,256]{1,0:T(8,128)}) %reduce-scatter.16.cloned.1.call-update) | async-done | bytes 524304 | tf_op jit(solution)/shard_map/reduce_scatter | solution.py:340
  1114.6 90.4 %reduce-scatter.18.cloned.1.call-done = f32[256,512]{1,0:T(8,128)} async-done(((f32[2048,512]{1,0:T(8,128)}), f32[256,512]{1,0:T(8,128)}) %reduce-scatter.18.cloned.1.call-update) | async-done | bytes 524304 | tf_op jit(solution)/shard_map/reduce_scatter | solution.py:341
  1206.8 165.5 %reduce-scatter.20.cloned.1.call-done = f32[9,64,512]{2,1,0:T(8,128)} async-done(((f32[9,512,512]{2,1,0:T(8,128)}), f32[9,64,512]{2,1,0:T(8,128)}) %reduce-scatter.20.cloned.1.call-update) | async-done | bytes 1179664 | tf_op jit(solution)/shard_map/reduce_scatter | solution.py:342
  1374.5 16.3 %add_convert_fusion = bf16[1568,2048]{1,0:T(8,128)(2,1)} fusion(f32[1568,2048]{1,0:T(8,128)} %get-tuple-element.267, f32[1568,2048]{1,0:T(8,128)} %add_divide_fusion.1, bf16[1568,512]{1,0:T(8,128)(2,1)} %convert_element_type.195, bf16[2048,512]{1,0:T(8,128)(2,1)} %all-gather.10.cloned.1.call-done), kind=kOutput, calls=%fused_computation.22 | convolution fusion | flops 3301179392 | bytes 35815424 | tf_op jit(solution)/shard_map/dot_general | solution.py:29
  1402.8 38.9 %all-reduce.70 = bf16[588,64]{1,0:T(8,128)(2,1)S(1)} all-reduce(f32[588,64]{1,0:T(8,128)S(1)} %reshape.293), channel_id=2, replica_groups=mesh['wide'=8,'narrow'=4] {'wide'}, use_global_device_ids=true, to_apply=%region_39.40.clone | all-reduce | flops 37632 | bytes 225792
  1442.6 58.3 %reduce-scatter.26.cloned.1.call-done = f32[64,9]{1,0:T(8,128)} async-done(((f32[512,9]{1,0:T(8,128)}), f32[64,9]{1,0:T(8,128)}) %reduce-scatter.26.cloned.1.call-update) | async-done | bytes 2320
  1501.7 13.6 all-reduce.64
  1517.2 33.8 %all-reduce.69.cloned.1.call-done = (bf16[256,512]{0,1:T(8,128)(2,1)}, bf16[512,256]{1,0:T(8,128)(2,1)}, bf16[256,512]{1,0:T(8,128)(2,1)}, bf16[9,64,512]{2,1,0:...) async-done(((bf16[256,512]{0,1:T(8,128)(2,1)}, bf16[512,256]{1,0:T(8,128)(2,1)}, bf16[256,512]{1,0:T(8,128)(2,1)}, bf16[9,64,512]{2,1,0:T(8,128)(2,1)}, ...) | async-done | bytes 1727504 | tf_op jit(solution)/shard_map/psum | solution.py:358
  (351 shorter events, 148.8 us)
Async XLA Ops:
  7.2 238.2 %all-gather.10.cloned.1.call-start = ((), (), s32[]{:S(2)}) async-start(), calls=%async_computation.8 | async-start | bytes 2359296 | tf_op jit(solution)/shard_map/all_gather | solution.py:159
  7.9 262.9 %all-gather.12.cloned.1.call-start = ((), (), s32[]{:S(2)}) async-start(), calls=%async_computation.9 | async-start | bytes 2359296 | tf_op jit(solution)/shard_map/all_gather | solution.py:162
  8.7 271.8 %all-gather.14.cloned.1.call-start = ((), (), s32[]{:S(2)}) async-start(), calls=%async_computation.10 | async-start | bytes 2359296 | tf_op jit(solution)/shard_map/all_gather | solution.py:163
  9.4 382.1 %all-gather.16.cloned.1.call-start = ((), (), s32[]{:S(2)}) async-start(), calls=%async_computation.11 | async-start | bytes 5308416 | tf_op jit(solution)/shard_map/all_gather | solution.py:166
  10.0 437.4 %all-gather.18.cloned.1.call-start = ((), (), s32[]{:S(2)}) async-start(), calls=%async_computation.12 | async-start | bytes 2359296 | tf_op jit(solution)/shard_map/all_gather | solution.py:169
  10.6 998.5 %reduce-scatter.24.cloned.1.call-start = ((), (), s32[]{:S(2)}) async-start(), calls=%async_computation.18 | async-start | bytes 1622016 | tf_op jit(solution)/shard_map/reduce_scatter | solution.py:344
  43.2 214.5 %copy-start.49 = (f32[1,512]{1,0:T(1,128)}, f32[1,512]{1,0:T(1,128)S(1)}, u32[]{:S(2)}) copy-start(f32[1,512]{1,0:T(1,128)S(1)} %get-tuple-element.236) | copy-start | bytes 6148
  43.2 214.5 %copy-start.51 = (f32[1,512]{1,0:T(1,128)}, f32[1,512]{1,0:T(1,128)S(1)}, u32[]{:S(2)}) copy-start(f32[1,512]{1,0:T(1,128)S(1)} %get-tuple-element.237) | copy-start | bytes 6148
  43.2 214.5 %copy-start.53 = (f32[1,512]{1,0:T(1,128)}, f32[1,512]{1,0:T(1,128)S(1)}, u32[]{:S(2)}) copy-start(f32[1,512]{1,0:T(1,128)S(1)} %get-tuple-element.238) | copy-start | bytes 6148
  43.2 214.5 %copy-start.55 = (f32[1,512]{1,0:T(1,128)}, f32[1,512]{1,0:T(1,128)S(1)}, u32[]{:S(2)}) copy-start(f32[1,512]{1,0:T(1,128)S(1)} %get-tuple-element.239) | copy-start | bytes 6148
  43.2 214.5 %copy-start.57 = (f32[1,512]{1,0:T(1,128)}, f32[1,512]{1,0:T(1,128)S(1)}, u32[]{:S(2)}) copy-start(f32[1,512]{1,0:T(1,128)S(1)} %get-tuple-element.240) | copy-start | bytes 6148
  43.2 214.5 %copy-start.59 = (f32[1,512]{1,0:T(1,128)}, f32[1,512]{1,0:T(1,128)S(1)}, u32[]{:S(2)}) copy-start(f32[1,512]{1,0:T(1,128)S(1)} %get-tuple-element.241) | copy-start | bytes 6148
  43.3 214.5 %copy-start.61 = (f32[1,512]{1,0:T(1,128)}, f32[1,512]{1,0:T(1,128)S(1)}, u32[]{:S(2)}) copy-start(f32[1,512]{1,0:T(1,128)S(1)} %get-tuple-element.242) | copy-start | bytes 6148
  43.3 214.5 %copy-start.63 = (f32[1,512]{1,0:T(1,128)}, f32[1,512]{1,0:T(1,128)S(1)}, u32[]{:S(2)}) copy-start(f32[1,512]{1,0:T(1,128)S(1)} %get-tuple-element.243) | copy-start | bytes 6148
  43.3 214.5 %copy-start.65 = (f32[1,512]{1,0:T(1,128)}, f32[1,512]{1,0:T(1,128)S(1)}, u32[]{:S(2)}) copy-start(f32[1,512]{1,0:T(1,128)S(1)} %get-tuple-element.244) | copy-start | bytes 6148
  74.1 190.4 %copy-start.33 = (f32[1,512]{1,0:T(1,128)}, f32[1,512]{1,0:T(1,128)S(1)}, u32[]{:S(2)}) copy-start(f32[1,512]{1,0:T(1,128)S(1)} %get-tuple-element.227) | copy-start | bytes 6148
  74.1 190.4 %copy-start.35 = (f32[1,512]{1,0:T(1,128)}, f32[1,512]{1,0:T(1,128)S(1)}, u32[]{:S(2)}) copy-start(f32[1,512]{1,0:T(1,128)S(1)} %get-tuple-element.229) | copy-start | bytes 6148
  74.2 190.4 %copy-start.37 = (f32[1,512]{1,0:T(1,128)}, f32[1,512]{1,0:T(1,128)S(1)}, u32[]{:S(2)}) copy-start(f32[1,512]{1,0:T(1,128)S(1)} %get-tuple-element.230) | copy-start | bytes 6148
  74.2 190.4 %copy-start.39 = (f32[1,512]{1,0:T(1,128)}, f32[1,512]{1,0:T(1,128)S(1)}, u32[]{:S(2)}) copy-start(f32[1,512]{1,0:T(1,128)S(1)} %get-tuple-element.231) | copy-start | bytes 6148
  74.2 190.4 %copy-start.41 = (f32[1,512]{1,0:T(1,128)}, f32[1,512]{1,0:T(1,128)S(1)}, u32[]{:S(2)}) copy-start(f32[1,512]{1,0:T(1,128)S(1)} %get-tuple-element.232) | copy-start | bytes 6148
  74.2 190.4 %copy-start.43 = (f32[1,512]{1,0:T(1,128)}, f32[1,512]{1,0:T(1,128)S(1)}, u32[]{:S(2)}) copy-start(f32[1,512]{1,0:T(1,128)S(1)} %get-tuple-element.233) | copy-start | bytes 6148
  74.2 190.4 %copy-start.45 = (f32[1,512]{1,0:T(1,128)}, f32[1,512]{1,0:T(1,128)S(1)}, u32[]{:S(2)}) copy-start(f32[1,512]{1,0:T(1,128)S(1)} %get-tuple-element.234) | copy-start | bytes 6148
  74.2 190.4 %copy-start.47 = (f32[1,512]{1,0:T(1,128)}, f32[1,512]{1,0:T(1,128)S(1)}, u32[]{:S(2)}) copy-start(f32[1,512]{1,0:T(1,128)S(1)} %get-tuple-element.235) | copy-start | bytes 6148
  74.2 190.4 %copy-start.67 = (f32[1,512]{1,0:T(1,128)}, f32[1,512]{1,0:T(1,128)S(1)}, u32[]{:S(2)}) copy-start(f32[1,512]{1,0:T(1,128)S(1)} %get-tuple-element.228) | copy-start | bytes 6148
  104.3 117.6 %copy-start.93 = (bf16[64]{0:T(256)(128)(2,1)}, bf16[64]{0:T(256)(128)(2,1)S(1)}, u32[]{:S(2)}) copy-start(bf16[64]{0:T(256)(128)(2,1)S(1)} %get-tuple-element.164) | copy-start | bytes 388
  185.9 37.1 %copy-start.23 = (bf16[32,32,32,3]{0,3,2,1:T(4,128)(2,1)S(1)}, bf16[32,32,32,3]{0,3,2,1:T(4,128)(2,1)}, u32[]{:S(2)}) copy-start(bf16[32,32,32,3]{0,3,2,1:T(4,128)(2,1)} %copy.95) | copy-start | bytes 589828
  190.3 48.9 %copy-start.27 = (bf16[32,32,32,3]{0,3,2,1:T(4,128)(2,1)}, bf16[32,32,32,3]{0,3,2,1:T(4,128)(2,1)S(1)}, u32[]{:S(2)}) copy-start(bf16[32,32,32,3]{0,3,2,1:T(4,128)(2,1)S(1)} %copy.98) | copy-start | bytes 589828
  256.5 8.0 copy-start.2
  270.8 9.7 copy-start.20
  514.9 49.0 %copy-start.79 = (f32[64]{0:T(128)S(1)}, f32[64]{0:T(128)}, u32[]{:S(2)}) copy-start(f32[64]{0:T(128)} %get-tuple-element.259) | copy-start | bytes 772
  515.0 49.8 %copy-start.86 = (s32[64]{0:T(128)S(1)}, s32[64]{0:T(128)}, u32[]{:S(2)}) copy-start(s32[64]{0:T(128)} %param.27) | copy-start | bytes 772
  564.1 21.2 %copy-start.73 = (f32[64]{0:T(128)}, f32[64]{0:T(128)S(1)}, u32[]{:S(2)}) copy-start(f32[64]{0:T(128)S(1)} %get-tuple-element.181) | copy-start | bytes 772
  564.8 20.6 %copy-start.88 = (f32[64]{0:T(128)}, f32[64]{0:T(128)S(1)}, u32[]{:S(2)}) copy-start(f32[64]{0:T(128)S(1)} %log.9) | copy-start | bytes 772
  624.5 10.5 copy-start.69
  624.5 10.5 copy-start.70
  624.5 10.5 copy-start.19
  624.5 10.5 copy-start.95
  747.5 263.1 %reduce-scatter.22.cloned.1.call-start = ((), (), s32[]{:S(2)}) async-start(), calls=%async_computation.17 | async-start | bytes 4718592 | tf_op jit(solution)/shard_map/reduce_scatter | solution.py:343
  794.9 10.8 copy-start.84
  805.6 215.3 %reduce-scatter.14.cloned.1.call-start = ((), (), s32[]{:S(2)}) async-start(), calls=%async_computation.13 | async-start | bytes 4718592 | tf_op jit(solution)/shard_map/reduce_scatter | solution.py:337
  836.4 24.5 %copy-start = (f32[4,8,7,7,512]{4,3,2,1,0:T(8,128)S(1)}, f32[4,8,7,7,512]{4,3,2,1,0:T(8,128)}, u32[]{:S(2)}) copy-start(f32[4,8,7,7,512]{4,3,2,1,0:T(8,128)} %reshape.291) | copy-start | bytes 9633796
  836.4 24.5 %copy-start.68 = (f32[1,512]{1,0:T(1,128)S(1)}, f32[1,512]{1,0:T(1,128)}, u32[]{:S(2)}) copy-start(f32[1,512]{1,0:T(1,128)} %copy-done.67) | copy-start | bytes 6148
  870.5 21.2 %copy-start.50 = (f32[1,512]{1,0:T(1,128)S(1)}, f32[1,512]{1,0:T(1,128)}, u32[]{:S(2)}) copy-start(f32[1,512]{1,0:T(1,128)} %copy-done.49) | copy-start | bytes 6148
  870.5 21.2 %copy-start.52 = (f32[1,512]{1,0:T(1,128)S(1)}, f32[1,512]{1,0:T(1,128)}, u32[]{:S(2)}) copy-start(f32[1,512]{1,0:T(1,128)} %copy-done.51) | copy-start | bytes 6148
  870.5 21.2 %copy-start.54 = (f32[1,512]{1,0:T(1,128)S(1)}, f32[1,512]{1,0:T(1,128)}, u32[]{:S(2)}) copy-start(f32[1,512]{1,0:T(1,128)} %copy-done.53) | copy-start | bytes 6148
  870.5 21.3 %copy-start.56 = (f32[1,512]{1,0:T(1,128)S(1)}, f32[1,512]{1,0:T(1,128)}, u32[]{:S(2)}) copy-start(f32[1,512]{1,0:T(1,128)} %copy-done.55) | copy-start | bytes 6148
  870.5 21.3 %copy-start.58 = (f32[1,512]{1,0:T(1,128)S(1)}, f32[1,512]{1,0:T(1,128)}, u32[]{:S(2)}) copy-start(f32[1,512]{1,0:T(1,128)} %copy-done.57) | copy-start | bytes 6148
  870.5 21.3 %copy-start.60 = (f32[1,512]{1,0:T(1,128)S(1)}, f32[1,512]{1,0:T(1,128)}, u32[]{:S(2)}) copy-start(f32[1,512]{1,0:T(1,128)} %copy-done.59) | copy-start | bytes 6148
  870.6 21.3 %copy-start.62 = (f32[1,512]{1,0:T(1,128)S(1)}, f32[1,512]{1,0:T(1,128)}, u32[]{:S(2)}) copy-start(f32[1,512]{1,0:T(1,128)} %copy-done.61) | copy-start | bytes 6148
  870.6 21.3 %copy-start.64 = (f32[1,512]{1,0:T(1,128)S(1)}, f32[1,512]{1,0:T(1,128)}, u32[]{:S(2)}) copy-start(f32[1,512]{1,0:T(1,128)} %copy-done.63) | copy-start | bytes 6148
  870.6 21.3 %copy-start.66 = (f32[1,512]{1,0:T(1,128)S(1)}, f32[1,512]{1,0:T(1,128)}, u32[]{:S(2)}) copy-start(f32[1,512]{1,0:T(1,128)} %copy-done.65) | copy-start | bytes 6148
  931.7 181.2 %reduce-scatter.16.cloned.1.call-start = ((), (), s32[]{:S(2)}) async-start(), calls=%async_computation.14 | async-start | bytes 4718592 | tf_op jit(solution)/shard_map/reduce_scatter | solution.py:340
  941.5 263.6 %reduce-scatter.18.cloned.1.call-start = ((), (), s32[]{:S(2)}) async-start(), calls=%async_computation.15 | async-start | bytes 4718592 | tf_op jit(solution)/shard_map/reduce_scatter | solution.py:341
  956.1 416.2 %reduce-scatter.20.cloned.1.call-start = ((), (), s32[]{:S(2)}) async-start(), calls=%async_computation.16 | async-start | bytes 10616832 | tf_op jit(solution)/shard_map/reduce_scatter | solution.py:342
  956.1 19.5 %copy-start.16 = (bf16[1568,512]{1,0:T(8,128)(2,1)S(1)}, bf16[1568,512]{1,0:T(8,128)(2,1)}, u32[]{:S(2)}) copy-start(bf16[1568,512]{1,0:T(8,128)(2,1)} %multiply_convert_fusion.4) | copy-start | bytes 4816900
  990.0 451.7 %reduce-scatter.28.cloned.1.call-start = ((), (), s32[]{:S(2)}) async-start(), calls=%async_computation.20 | async-start | bytes 294912
  991.8 509.1 %reduce-scatter.26.cloned.1.call-start = ((), (), s32[]{:S(2)}) async-start(), calls=%async_computation.19 | async-start | bytes 294912
  992.8 558.3 %all-reduce.69.cloned.1.call-start = ((), (), s32[]{:S(2)}) async-start(), calls=%async_computation.21 | async-start | bytes 3457024 | tf_op jit(solution)/shard_map/psum | solution.py:358
  1374.5 25.2 %copy-start.30 = (f32[64,174]{1,0:T(8,128)S(1)}, f32[64,174]{1,0:T(8,128)}, u32[]{:S(2)}) copy-start(f32[64,174]{1,0:T(8,128)} %copy-done.29) | copy-start | bytes 133636
  1374.5 25.2 %copy-start.74 = (f32[64]{0:T(128)S(1)}, f32[64]{0:T(128)}, u32[]{:S(2)}) copy-start(f32[64]{0:T(128)} %copy-done.73) | copy-start | bytes 772
  1374.5 25.2 %copy-start.87 = (s32[64]{0:T(128)S(1)}, s32[64]{0:T(128)}, u32[]{:S(2)}) copy-start(s32[64]{0:T(128)} %param.27) | copy-start | bytes 772
  1374.5 25.2 %copy-start.89 = (f32[64]{0:T(128)S(1)}, f32[64]{0:T(128)}, u32[]{:S(2)}) copy-start(f32[64]{0:T(128)} %copy-done.88) | copy-start | bytes 772
  1374.5 26.6 %copy-start.10 = (bf16[8192,64]{1,0:T(8,128)(2,1)S(1)}, bf16[8192,64]{1,0:T(8,128)(2,1)}, u32[]{:S(2)}) copy-start(bf16[8192,64]{1,0:T(8,128)(2,1)} %get-tuple-element.201) | copy-start | bytes 3145732
  1551.0 8.6 copy-start.32
  (46 other events, 188.9 us)
Sparse Core Ops, SparseCore 0:
  10.2 52.3 all-gather.9
  64.6 49.5 all-gather.11
  116.3 52.8 all-gather.13
  171.2 79.1 all-gather.15
  252.3 47.5 all-gather.17
  747.6 65.4 reduce-scatter.23
  816.7 86.7 reduce-scatter.21
  931.8 89.1 reduce-scatter.13
  1024.6 88.2 reduce-scatter.15
  1117.4 87.6 reduce-scatter.17
  1208.7 163.5 reduce-scatter.19
  1376.0 60.4 reduce-scatter.27
  1440.4 60.4 reduce-scatter.25
  1505.2 45.7 all-reduce.68
where the time goes:
time: 1580 us; the launch traced here: 1570 us
  blocking collectives  519 us (33%)
  waiting for transfers between devices  450 us (28%)
  other arithmetic  212 us (13%)
  matrix products  199 us (13%)
  local copies, waits for them, and re-layouts  168 us (11%)
  between operations  19.8 us (1%)
    reduce_scatter x1, waiting for transfers between devices, shards(): lax.psum_scatter(spatial_grad, 'wide', scatter_dimension=1, tiled=True)  165 us
    psum x4, blocking collectives, norm_forward(): lax.psum((jnp.sum(values, 0), jnp.sum(values * values, 0)), ('wide', 'nar...  160 us
    reduce_scatter x1, waiting for transfers between devices, shards(): lax.psum_scatter(reduce_grad, 'wide', scatter_dimension=0, tiled=True)  90.4 us
    reduce_scatter x1, waiting for transfers between devices, shards(): lax.psum_scatter(expand_grad, 'wide', scatter_dimension=1, tiled=True)  90.1 us
    psum x2, blocking collectives, norm_backward(): lax.psum((jnp.sum(grad, 0), jnp.sum(grad * unit, 0)), ('wide', 'narrow'))  77.9 us
    dot_general x6, matrix products, product_right(): lax.dot_general(first_operand, second_operand, (((1,), (1,)), ((), ())),...  64.4 us
    unnamed x16, waiting for transfers between devices  61.5 us
    unnamed x2, blocking collectives  61.2 us
  transfers between devices with their start and end apart: 14, of which 6 were waited for; matrix products, arithmetic and copies ran while one was open for 27% of the time, Pallas kernels for 0%

commit v1 on v0

v1 whole, which is shorter than its diff:
```python
import jax
import jax.numpy as jnp
from jax import lax
from jax.sharding import PartitionSpec as P

C = 2048
B = 512
R = 512
CLASSES = 174
SEG = 8
SIDE = 7
PER_VIEW = SEG * SIDE * SIDE

epsilon = 1e-05
loss_scale = 1024.0

AXES = ("wide", "narrow")
f32 = jnp.float32
bf16 = jnp.bfloat16


def product(first_operand, second_operand):
    return jnp.dot(first_operand, second_operand, preferred_element_type=f32)


def product_left(first_operand, second_operand):
    return lax.dot_general(
        first_operand, second_operand, (((0,), (0,)), ((), ())), preferred_element_type=f32
    )


def product_right(first_operand, second_operand):
    return lax.dot_general(
        first_operand, second_operand, (((1,), (1,)), ((), ())), preferred_element_type=f32
    )


def bit_count(size):
    return size.bit_length() - 1


def device_bits():
    return bit_count(lax.axis_size(AXES))


def exchange(values, mask):
    size = lax.axis_size(AXES)
    return lax.ppermute(values, AXES, [(index, index ^ mask) for index in range(size)])


def own_bit(bit):
    return (lax.axis_index(AXES) >> bit) & 1


def total(values):
    bits = device_bits()
    values = values + exchange(values, 1)
    for bit in range(1, bits, 2):
        masks = [1 << bit]
        if bit + 1 < bits:
            masks += [2 << bit, 3 << bit]
        parts = [exchange(values, mask) for mask in masks]
        for part in parts:
            values = values + part
    return values


def total_of(*arrays):
    flat = jnp.concatenate([array.reshape(-1) for array in arrays])
    flat = total(flat)
    found, at = [], 0
    for array in arrays:
        found.append(flat[at : at + array.size].reshape(array.shape))
        at += array.size
    return found


def gather_tree(block, order, lead=0):
    done = []
    for bit in order:
        other = exchange(block, 1 << bit)
        low = own_bit(bit) == 0
        place = lead + sum(1 for known in done if known > bit)
        block = jnp.stack(
            [jnp.where(low, block, other), jnp.where(low, other, block)], axis=place
        )
        done.append(bit)
    shape = block.shape
    return block.reshape(shape[:lead] + (1 << len(done),) + shape[lead + len(done) :])


def scatter_tree(values, order, lead=0):
    shape = values.shape
    values = values.reshape(shape[:lead] + (2,) * len(order) + shape[lead + 1 :])
    left = sorted(order, reverse=True)
    for bit in order:
        place = lead + left.index(bit)
        mine = own_bit(bit)
        keep = lax.dynamic_index_in_dim(values, mine, place, keepdims=False)
        send = lax.dynamic_index_in_dim(values, 1 - mine, place, keepdims=False)
        values = keep + exchange(send, 1 << bit)
        left.remove(bit)
    return values


def own_part(values, axis):
    width = values.shape[axis] // lax.axis_size("narrow")
    return lax.dynamic_slice_in_dim(values, lax.axis_index("narrow") * width, width, axis)


def own_slice(values, width):
    return lax.dynamic_slice_in_dim(values, lax.axis_index("wide") * width, width)


def depthwise(feature, kernel):
    extent = feature.shape[2]
    padded = jnp.pad(feature, ((0, 0), (0, 0), (1, 1), (1, 1), (0, 0)))
    accumulated = jnp.zeros_like(feature)
    for offset in range(9):
        accumulated = (
            accumulated
            + padded[:, :, offset // 3 : offset // 3 + extent, offset % 3 : offset % 3 + extent, :]
            * kernel[offset]
        )
    return accumulated


def temporal(squeezed, next_kernel, scale_kernel):
    upcoming = jnp.concatenate([squeezed[:, 1:], jnp.zeros_like(squeezed[:, :1])], axis=1)
    differ = depthwise(upcoming, next_kernel) - squeezed
    return differ + depthwise(differ, scale_kernel) + jnp.mean(differ, axis=(2, 3), keepdims=True)


def columns(feature):
    extent = feature.shape[2]
    padded = jnp.pad(feature, ((0, 0), (0, 0), (1, 1), (1, 1), (0, 0)))
    pieces = [
        padded[:, :, offset // 3 : offset // 3 + extent, offset % 3 : offset % 3 + extent, :]
        for offset in range(9)
    ]
    return jnp.concatenate(pieces, axis=-1).reshape(-1, 9 * feature.shape[-1])


def frame_differ(frames):
    differ = jnp.concatenate(
        [frames[:, :, index + 1] - frames[:, :, index] for index in range(4)], axis=-1
    )
    return differ.reshape((-1,) + differ.shape[2:])


def stem_conv(differ, kernel):
    return lax.conv_general_dilated(
        differ,
        kernel,
        (2, 2),
        ((3, 3), (3, 3)),
        dimension_numbers=("NHWC", "HWIO", "NHWC"),
        preferred_element_type=f32,
    )


def silu_slope(values):
    sigma = jax.nn.sigmoid(values)
    return sigma * (1.0 + values * (1.0 - sigma))


def moments(values):
    return jnp.sum(values, 0), jnp.sum(values * values, 0)


def normalize(values, sums, squares, gain, shift, count):
    mean = sums / count
    inverse = lax.rsqrt(squares / count - mean * mean + epsilon)
    unit = (values - mean) * inverse
    return unit * gain + shift, unit, inverse


def grad_moments(grad, unit):
    return jnp.sum(grad, 0), jnp.sum(grad * unit, 0)


def input_grad(grad, unit, inverse, gain, shift_grad, gain_grad, count):
    return gain * inverse * (grad - shift_grad / count - unit * gain_grad / count)


def shards(
    frames,
    tokens,
    stem_cotangent,
    crop_counts,
    labels,
    stem_weight,
    stem_gain,
    stem_shift,
    w_squeeze,
    next_kernel,
    scale_kernel,
    w_expand,
    w_reduce,
    gain_one,
    shift_one,
    w_spatial,
    gain_two,
    shift_two,
    w_restore,
    gain_three,
    shift_three,
    w_class,
    class_bias,
):
    view_count = frames.shape[0]
    row_count = tokens.shape[0]
    devices = lax.axis_size(AXES)
    wide = lax.axis_size("wide")
    narrow = lax.axis_size("narrow")
    count = float(row_count * devices)
    bits = device_bits()
    outward = list(reversed(range(bits)))
    wide_bits = [bit for bit in outward if bit >= bit_count(narrow)]
    narrow_bits = [bit for bit in outward if bit < bit_count(narrow)]

    small = [
        stem_weight, stem_gain, stem_shift, next_kernel, scale_kernel, gain_one, shift_one,
        gain_two, shift_two, gain_three, shift_three,
    ]
    pack = jnp.concatenate([value.reshape(-1) for value in small])
    pack = jnp.pad(pack, (0, -pack.size % 1024))
    packs = gather_tree(pack.reshape(-1, 128), wide_bits).reshape(wide, -1)
    full, at = [], 0
    for value in small:
        piece = packs[:, at : at + value.size].reshape((wide,) + value.shape)
        at += value.size
        full.append(
            piece.reshape(-1)
            if value.ndim == 1
            else piece.transpose(1, 0, 2).reshape(value.shape[0], -1)
        )
    full_stem = full[0]
    (
        full_stem_gain, full_stem_shift, full_next, full_scale, full_gain_one, full_shift_one,
        full_gain_two, full_shift_two, full_gain_three, full_shift_three,
    ) = (value.astype(f32) for value in full[1:])

    full_squeeze = gather_tree(own_part(w_squeeze, 0), outward).reshape(C, R)
    full_expand = gather_tree(own_part(w_expand, 0), outward)
    full_expand = full_expand.reshape(wide, R, -1).transpose(1, 0, 2).reshape(R, C)
    full_reduce = gather_tree(own_part(w_reduce, 0), outward).reshape(C, B)
    full_spatial = gather_tree(own_part(w_spatial, 1), outward, 1).reshape(9 * B, B)
    full_restore = gather_tree(own_part(w_restore, 0), outward).reshape(B, C)
    full_class = gather_tree(own_part(w_class, 0), outward).reshape(C, CLASSES)

    differ_low = frame_differ(frames.astype(f32)).astype(bf16)
    stem_width_all = full_stem.shape[1]
    stem_kernel = full_stem.reshape(7, 7, differ_low.shape[-1], stem_width_all)
    stem_pre = stem_conv(differ_low, stem_kernel).reshape(-1, stem_width_all)
    stem_count = float(stem_pre.shape[0] * devices)

    squeezed = product(tokens, full_squeeze)

    def mixing(squeezed_values, next_values, scale_values):
        return temporal(
            squeezed_values.reshape(view_count, SEG, SIDE, SIDE, R), next_values, scale_values
        ).reshape(row_count, R)

    mixed, mixing_back = jax.vjp(mixing, squeezed, full_next, full_scale)
    mixed_low = mixed.astype(bf16)
    gate = jax.nn.sigmoid(product(mixed_low, full_expand))
    token_values = tokens.astype(f32)
    gated = token_values + token_values * gate
    gated_low = gated.astype(bf16)
    pre_one = product(gated_low, full_reduce)

    one_sums, one_squares, stem_sums, stem_squares = total_of(
        *moments(pre_one), *moments(stem_pre)
    )
    norm_one, unit_one, inverse_one = normalize(
        pre_one, one_sums, one_squares, full_gain_one, full_shift_one, count
    )
    stem_norm, stem_unit, stem_inverse = normalize(
        stem_pre, stem_sums, stem_squares, full_stem_gain, full_stem_shift, stem_count
    )
    stem_out = jax.nn.silu(stem_norm)
    stem_norm_grad = stem_cotangent.astype(f32) * silu_slope(stem_norm)

    hidden_one = jax.nn.silu(norm_one).astype(bf16)
    spread_cols = columns(hidden_one.reshape(view_count, SEG, SIDE, SIDE, B))
    pre_two = product(spread_cols, full_spatial)
    two_sums, two_squares = total_of(*moments(pre_two))
    norm_two, unit_two, inverse_two = normalize(
        pre_two, two_sums, two_squares, full_gain_two, full_shift_two, count
    )
    hidden_two = jax.nn.silu(norm_two).astype(bf16)
    pre_three = product(hidden_two, full_restore)
    three_sums, three_squares, stem_shift_grad, stem_gain_grad = total_of(
        *moments(pre_three), *grad_moments(stem_norm_grad, stem_unit)
    )
    norm_three, unit_three, inverse_three = normalize(
        pre_three, three_sums, three_squares, full_gain_three, full_shift_three, count
    )
    summed = norm_three + gated
    output = jax.nn.silu(summed)
    pooled = jnp.mean(output.reshape(view_count, PER_VIEW, C), 1)
    pooled_low = pooled.astype(bf16)
    view_logits = product(pooled_low, full_class) + class_bias.astype(f32)

    ends = jnp.cumsum(crop_counts)
    starts = ends - crop_counts
    index = lax.axis_index(AXES)
    positions = (index - 1) * view_count + jnp.arange(3 * view_count, dtype=jnp.int32)
    video = jnp.sum((ends[None, :] <= positions[:, None]).astype(jnp.int32), 1)
    own_video = video[view_count : 2 * view_count]
    belongs = (
        own_video[:, None] == jnp.arange(crop_counts.shape[0], dtype=jnp.int32)[None, :]
    ).astype(jnp.int32)
    own_count = jnp.sum(belongs * crop_counts[None, :], 1).astype(f32)
    own_label = jnp.sum(belongs * labels[None, :], 1)
    own_start = jnp.sum(belongs * starts[None, :], 1)
    first = (own_start == positions[view_count : 2 * view_count]).astype(f32)
    same = (own_video[:, None] == video[None, :]).astype(f32) / own_count[:, None]
    target = (own_label[:, None] == jnp.arange(CLASSES, dtype=jnp.int32)[None, :]).astype(f32)

    before = lax.ppermute(view_logits, AXES, [(i, i + 1) for i in range(devices - 1)])
    after = lax.ppermute(view_logits, AXES, [(i + 1, i) for i in range(devices - 1)])
    near = jnp.concatenate([before, view_logits, after])
    video_logits = jnp.sum(same[:, :, None] * near[None, :, :], 1)
    log_probs = jax.nn.log_softmax(video_logits, axis=-1)
    entropy_part = jnp.sum(first * -jnp.sum(target * log_probs, axis=-1))
    video_grad = loss_scale * (jnp.exp(log_probs) - target)
    bias_part = jnp.sum(first[:, None] * video_grad, 0)
    view_grad_low = (video_grad / own_count[:, None]).astype(bf16)

    class_grad = product_left(pooled_low, view_grad_low)
    pooled_grad = product_right(view_grad_low, full_class)
    output_grad = jnp.broadcast_to(
        (pooled_grad / PER_VIEW)[:, None, :], (view_count, PER_VIEW, C)
    ).reshape(row_count, C)
    summed_grad = output_grad * silu_slope(summed)
    shift_three_grad, gain_three_grad, class_bias_grad, entropy_sum = total_of(
        *grad_moments(summed_grad, unit_three), bias_part, entropy_part
    )
    loss = entropy_sum / crop_counts.shape[0]
    low_three = input_grad(
        summed_grad, unit_three, inverse_three, full_gain_three, shift_three_grad,
        gain_three_grad, count,
    ).astype(bf16)
    restore_grad = product_left(hidden_two, low_three)
    hidden_two_grad = product_right(low_three, full_restore)
    norm_two_grad = hidden_two_grad * silu_slope(norm_two)
    shift_two_grad, gain_two_grad = total_of(*grad_moments(norm_two_grad, unit_two))
    low_two = input_grad(
        norm_two_grad, unit_two, inverse_two, full_gain_two, shift_two_grad, gain_two_grad, count
    ).astype(bf16)
    spatial_grad = product_left(spread_cols, low_two).reshape(9, -1, B)
    cols_grad = product_right(low_two, full_spatial)
    spread_back = jax.vjp(columns, jnp.zeros((view_count, SEG, SIDE, SIDE, B), f32))[1]
    hidden_one_grad = spread_back(cols_grad)[0].reshape(row_count, B)
    norm_one_grad = hidden_one_grad * silu_slope(norm_one)
    shift_one_grad, gain_one_grad = total_of(*grad_moments(norm_one_grad, unit_one))
    low_one = input_grad(
        norm_one_grad, unit_one, inverse_one, full_gain_one, shift_one_grad, gain_one_grad, count
    ).astype(bf16)
    reduce_grad = product_left(gated_low, low_one)
    gated_grad = product_right(low_one, full_reduce) + summed_grad
    gate_logit_grad = (gated_grad * token_values * gate * (1.0 - gate)).astype(bf16)
    expand_grad = product_left(mixed_low, gate_logit_grad)
    mixed_grad = product_right(gate_logit_grad, full_expand)
    squeezed_grad, next_grad, scale_grad = mixing_back(mixed_grad)
    low_squeezed = squeezed_grad.astype(bf16)
    squeeze_grad = product_left(tokens, low_squeezed)
    tokens_grad = (gated_grad * (1.0 + gate) + product_right(low_squeezed, full_squeeze)).astype(
        bf16
    )
    stem_pre_low = input_grad(
        stem_norm_grad, stem_unit, stem_inverse, full_stem_gain, stem_shift_grad, stem_gain_grad,
        stem_count,
    ).astype(bf16).astype(f32)
    differ_values = differ_low.astype(f32)

    def stem_map(kernel_values):
        return stem_conv(differ_values, kernel_values)

    stem_map_back = jax.vjp(stem_map, stem_kernel.astype(f32))[1]
    stem_grad = stem_map_back(
        stem_pre_low.reshape(
            differ_low.shape[0], differ_low.shape[1] // 2, differ_low.shape[2] // 2, stem_width_all
        )
    )[0].reshape(-1, stem_width_all)

    inward = list(range(bits))

    def reduced(grad, lead):
        shape = grad.shape
        rows = shape[lead] // devices
        parts = grad.astype(bf16).reshape(shape[:lead] + (devices, rows) + shape[lead + 1 :])
        part = scatter_tree(parts, inward, lead)
        whole = gather_tree(part, narrow_bits, lead)
        return whole.reshape(shape[:lead] + (narrow * rows,) + shape[lead + 1 :]).astype(f32)

    sum_restore = reduced(restore_grad, 0)
    sum_class = reduced(class_grad, 0)
    sum_spatial = reduced(spatial_grad, 1)
    sum_reduce = reduced(reduce_grad, 0)
    tiles = expand_grad.reshape(R, wide, -1).transpose(1, 0, 2)
    sum_expand = reduced(tiles.reshape(wide * R, -1), 0)
    sum_squeeze = reduced(squeeze_grad, 0)

    def cut(grad):
        return grad.reshape(grad.shape[0], wide, -1).transpose(1, 0, 2).reshape(wide, -1)

    cuts = [cut(stem_grad), cut(next_grad), cut(scale_grad)]
    joined = jnp.concatenate(cuts, 1)
    joined = jnp.pad(joined, ((0, 0), (0, -joined.shape[1] % 1024))).astype(bf16)
    parts = joined.reshape(wide, -1, 128)
    for bit in narrow_bits:
        parts = parts + exchange(parts, 1 << bit)
    mine = scatter_tree(parts, list(reversed(wide_bits))).reshape(-1).astype(f32)
    sizes = [piece.shape[1] for piece in cuts]
    sum_stem = mine[: sizes[0]].reshape(stem_weight.shape)
    sum_next = mine[sizes[0] : sizes[0] + sizes[1]].reshape(next_kernel.shape)
    sum_scale = mine[sizes[0] + sizes[1] : sum(sizes)].reshape(scale_kernel.shape)

    stem_width = stem_gain.shape[0]
    inner_width = gain_one.shape[0]
    outer_width = gain_three.shape[0]
    return (
        output.astype(bf16),
        stem_out.astype(bf16),
        tokens_grad,
        sum_stem,
        own_slice(stem_gain_grad, stem_width),
        own_slice(stem_shift_grad, stem_width),
        sum_squeeze,
        sum_next,
        sum_scale,
        sum_expand,
        sum_reduce,
        own_slice(gain_one_grad, inner_width),
        own_slice(shift_one_grad, inner_width),
        sum_spatial,
        own_slice(gain_two_grad, inner_width),
        own_slice(shift_two_grad, inner_width),
        sum_restore,
        own_slice(gain_three_grad, outer_width),
        own_slice(shift_three_grad, outer_width),
        sum_class,
        class_bias_grad,
        loss,
    )


def solution(mesh):
    in_specs = (
        P(("wide", "narrow"), None, None, None, None, None),
        P(("wide", "narrow"), None),
        P(("wide", "narrow"), None),
        P(),
        P(),
        P(None, "wide"),
        P("wide"),
        P("wide"),
        P("wide", None),
        P(None, "wide"),
        P(None, "wide"),
        P(None, "wide"),
        P("wide", None),
        P("wide"),
        P("wide"),
        P(None, "wide", None),
        P("wide"),
        P("wide"),
        P("wide", None),
        P("wide"),
        P("wide"),
        P("wide", None),
        P(),
    )
    out_specs = (
        P(("wide", "narrow"), None),
        P(("wide", "narrow"), None),
        P(("wide", "narrow"), None),
        P(None, "wide"),
        P("wide"),
        P("wide"),
        P("wide", None),
        P(None, "wide"),
        P(None, "wide"),
        P(None, "wide"),
        P("wide", None),
        P("wide"),
        P("wide"),
        P(None, "wide", None),
        P("wide"),
        P("wide"),
        P("wide", None),
        P("wide"),
        P("wide"),
        P("wide", None),
        P(),
        P(),
    )
    return jax.shard_map(shards, mesh=mesh, in_specs=in_specs, out_specs=out_specs, check_vma=False)
```

time: 1580 us -> 967 us (0.61)
  blocking collectives: 519 us -> 0 us
  waiting for transfers between devices: 450 us -> 185 us
  starting transfers between devices: 0.77 us -> 132 us
  local copies, waits for them, and re-layouts: 168 us -> 223 us
    reduce_scatter x6 -> x0, waiting for transfers between devices: 355 us -> none  [the longest x1 165 us: shards(): lax.psum_scatter(spatial_grad, 'wide', scatter_dimension=1, tiled=True)]
    psum x8 -> x0, blocking collectives: 293 us -> none  [the longest x4 160 us: norm_forward(): lax.psum((jnp.sum(values, 0), jnp.sum(values * values, 0)), ('wide', 'nar...]
    ppermute x0 -> x124, waiting for transfers between devices: none -> 185 us  [the longest x122 185 us: exchange(): lax.ppermute(values, AXES, [(index, index ^ mask) for index in range(size)])]
    all_gather x6 -> x0, blocking collectives: 165 us -> none  [the longest x1 35.6 us: shards(): lax.all_gather(w_class, 'wide', axis=0, tiled=True)]
    ppermute x0 -> x124, starting transfers between devices: none -> 132 us  [the longest x122 127 us: exchange(): lax.ppermute(values, AXES, [(index, index ^ mask) for index in range(size)])]
    unnamed x16 -> x0, waiting for transfers between devices: 61.5 us -> none
    unnamed x2 -> x0, blocking collectives: 61.2 us -> none
    psum x1 -> x0, waiting for transfers between devices: 33.8 us -> none  [shards(): lax.psum(part_squeeze.astype(jnp.bfloat16), 'narrow').astype(jnp.float32)]
  transfers between devices with their start and end apart: 14 -> 124, of which waited for: 6 -> 48; matrix products, arithmetic and copies ran while one was open for 27% -> 58% of each run, Pallas kernels for 0% -> 0%
where the time goes in v1:
time: 967 us; the launch traced here: 958 us
  local copies, waits for them, and re-layouts  223 us (23%)
  matrix products  208 us (22%)
  other arithmetic  204 us (21%)
  waiting for transfers between devices  185 us (19%)
  starting transfers between devices  132 us (14%)
    ppermute x122, waiting for transfers between devices, exchange(): lax.ppermute(values, AXES, [(index, index ^ mask) for index in range(size)])  185 us
    ppermute x122, starting transfers between devices, exchange(): lax.ppermute(values, AXES, [(index, index ^ mask) for index in range(size)])  127 us
    dot_general x6, matrix products, product_right(): lax.dot_general(first_operand, second_operand, (((1,), (1,)), ((), ())),...  85 us
    dot_general x6, matrix products, product_left(): lax.dot_general(first_operand, second_operand, (((0,), (0,)), ((), ())),...  47.3 us
    conv_general_dilated x2, matrix products, stem_conv(): lax.conv_general_dilated(differ, kernel, (2, 2), ((3, 3), (3, 3)), dimens...  44.6 us
    dot_general x6, matrix products, product(): return jnp.dot(first_operand, second_operand, preferred_element_type=f32)  31.1 us
    concatenate x9, local copies, waits for them, and re-layouts, columns(): return jnp.concatenate(pieces, axis=-1).reshape(-1, 9 * feature.shape[-1])  29.7 us
    unnamed x338, local copies, waits for them, and re-layouts  29.7 us
  transfers between devices with their start and end apart: 124, of which 48 were waited for; matrix products, arithmetic and copies ran while one was open for 58% of the time, Pallas kernels for 0%

profile of v1, /device:TPU:0, one launch (start us, length us, event | category | flops | bytes accessed | tf_op | source)
XLA Modules:
  0.0 957.5 jit_solution(3423850379196096149)
XLA Ops:
  1.7 4.1 collective-permute-start.49
  15.8 5.4 concatenate.57
  50.2 4.0 collective-permute-start.25
  74.2 34.2 %multiply_reduce_fusion.3 = (f32[64]{0:T(128)S(1)}, f32[64]{0:T(128)S(1)}, f32[32,16,16,64]{3,0,2,1:T(8,128)}) fusion(bf16[7,7,12,64]{2,1,0,3:T(8,128)(2,1)S(1)} %reshape_reshape.54, bf16[32,32,32,3]{0,3,2,1:T(4,128)(2,1)} %copy.355, bf16[32,32,32,3]{0,3,2,1:T(4,128)(2,1)S(1)} %copy-done.65, bf16[32,32,32,3]{0,3,2,1:T(4,128)(2,1)} %copy.353, ...), kind=kOutput, calls=%fused_computation.57 | convolution fusion | flops 556990336 | bytes 2959360 | tf_op jit(solution)/shard_map/conv_general_dilated | solution.py:152
  111.4 6.8 copy.364
  119.9 3.9 collective-permute-done.51
  152.8 13.4 %collective-permute-done.16 = bf16[2,2,2,64,512]{4,3,2,1,0:T(8,128)(2,1)S(1)} collective-permute-done((bf16[2,2,2,64,512]{4,3,2,1,0:T(8,128)(2,1)S(1)}, bf16[2,2,2,64,512]{4,3,2,1,0:T(8,128)(2,1)S(1)}, u32[]{:S(2)}, u32[]{:S(2)}) %collective-permute-start.16) | collective-permute-done | bytes 524320 | tf_op jit(solution)/shard_map/ppermute | solution.py:48
  167.9 9.6 %collective-permute-done.11 = bf16[2,2,2,128,256]{4,3,2,1,0:T(8,128)(2,1)S(1)} collective-permute-done((bf16[2,2,2,128,256]{4,3,2,1,0:T(8,128)(2,1)S(1)}, bf16[2,2,2,128,256]{4,3,2,1,0:T(8,128)(2,1)S(1)}, u32[]{:S(2)}, u32[]{:S(2)}) %collective-permute-start.11) | collective-permute-done | bytes 524320 | tf_op jit(solution)/shard_map/ppermute | solution.py:48
  177.7 8.9 collective-permute-done.3
  209.1 4.2 fusion.64
  215.1 4.8 add_convert_fusion.2
  223.6 6.9 add_divide_fusion.1
  230.6 5.5 multiply_reduce_fusion.25
  257.4 12.1 %pad_slice_fusion.16 = (bf16[4,8,7,7,512]{4,3,2,1,0:T(8,128)(2,1)}, bf16[4,8,7,7,512]{4,3,2,1,0:T(8,128)(2,1)}, bf16[4,8,7,7,512]{4,3,2,1,0:T(8,128)(2,1)}, bf16...) fusion(bf16[4,8,7,7,512]{4,3,2,1,0:T(8,128)(2,1)} %reshape.511), kind=kLoop, calls=%fused_computation.31 | loop fusion | bytes 14450688 | tf_op jit(solution)/shard_map/slice | solution.py:138
  269.4 3.7 concatenate.67
  273.1 3.8 concatenate.61
  288.0 3.7 concatenate.65
  313.0 7.7 fusion.58
  336.8 7.1 multiply_reduce_fusion.1
  357.0 17.7 %fusion.62 = (bf16[1568,2048]{1,0:T(8,128)(2,1)}, f32[1568,2048]{1,0:T(8,128)}) fusion(f32[1568,2048]{1,0:T(8,128)} %copy-done.2, bf16[1568,2048]{1,0:T(8,128)(2,1)} %param.24, f32[2048]{0:T(1024)S(1)} %bitcast.612, f32[2048]{0:T(1024)S(1)} %bitcast.608, f32[2048]{0:T(1024)S(1)} %get-tuple-element.350, f32[1568,2048]{1,0:T(8,128)} %get-tuple-element.368, ...), kind=kLoop, calls=%fused_computation.491 | loop fusion | flops 41746432 | bytes 51412992 | tf_op jit(solution)/shard_map/convert_element_type | solution.py:426
  374.7 5.4 reduce_sum.428
  384.9 3.7 reshape.548
  391.1 4.2 reshape.547
  395.4 19.4 %copy.389 = bf16[4608,1568]{1,0:T(8,128)(2,1)} copy(bf16[4608,1568]{0,1:T(8,128)(2,1)} %bitcast.561) | data formatting | bytes 28901376 | tf_op jit(solution)/shard_map/dot_general | solution.py:27
  416.5 17.7 %multiply_reduce_fusion = (f32[2048]{0:T(1024)S(1)}, f32[2048]{0:T(1024)S(1)}, f32[1568,2048]{1,0:T(8,128)}) fusion(f32[1568,2048]{1,0:T(8,128)} %get-tuple-element.368, f32[2048]{0:T(1024)S(1)} %get-tuple-element.350, f32[2048]{0:T(1024)S(1)} %get-tuple-element.351, f32[1568,2048]{1,0:T(8,128)} %copy-done.2, bf16[1568,2048]{1,0:T(8,128)(2,1)} %param.24, ...), kind=kLoop, calls=%fused_computation.24 | loop fusion | flops 61009920 | bytes 45039616 | tf_op jit(solution)/shard_map/reduce_sum | solution.py:179
  440.7 5.9 multiply_convert_fusion.1
  451.2 10.4 %fusion.23 = bf16[7,7,12,64]{3,2,1,0:T(8,128)(2,1)S(1)} fusion(bf16[32,16,16,64]{3,2,1,0:T(8,128)(2,1)S(1)} %bitcast.593, bf16[32,32,32,3]{0,3,2,1:T(4,128)(2,1)S(1)} %copy-done.70, bf16[32,32,32,3]{0,3,2,1:T(4,128)(2,1)S(1)} %copy-done.66, bf16[32,32,32,3]{0,3,2,1:T(4,128)(2,1)S(1)} %copy-done.69, bf16[32,32,32,3]{0,3,2,1:T(4,128)(2,1)S(1)} %copy-done.68), kind=kOutput, calls=%fused_computation.163 | convolution fusion | flops 555455232 | bytes 1910272 | tf_op jit(solution)/shard_map/transpose(jvp())/conv_general_dilated | solution.py:152
  468.3 10.5 %multiply_convert_fusion = bf16[1568,2048]{1,0:T(8,128)(2,1)S(1)} fusion(f32[1568,2048]{1,0:T(8,128)} %get-tuple-element.196, f32[1568,2048]{1,0:T(8,128)} %get-tuple-element.368, f32[2048]{0:T(1024)S(1)} %get-tuple-element.345, f32[2048]{0:T(1024)S(1)} %get-tuple-element.344, f32[2048]{0:T(1024)S(1)} %get-tuple-element.349, ...), kind=kLoop, calls=%fused_computation.23 | loop fusion | flops 25690112 | bytes 32153600 | tf_op jit(solution)/shard_map/convert_element_type | solution.py:345
  478.8 6.9 fusion.57
  497.8 9.6 %convolution_convert_fusion = bf16[512,2048]{1,0:T(8,128)(2,1)} fusion(bf16[1568,2048]{1,0:T(8,128)(2,1)} %copy-done.34, f32[1568,512]{1,0:T(8,128)} %copy-done.46, f32[512]{0:T(512)S(1)} %reshape.532, f32[512]{0:T(512)S(1)} %reshape.531, f32[512]{0:T(512)S(1)} %get-tuple-element.363, f32[512]{0:T(512)S(1)} %get-tuple-element.364), kind=kOutput, calls=%fused_computation.115 | convolution fusion | flops 3296608256 | bytes 11739136 | tf_op jit(solution)/shard_map/dot_general | solution.py:27
  509.8 15.7 %fusion.19 = f32[4,8,7,7,4608]{4,1,3,2,0:T(8,128)} fusion(bf16[4608,512,1,1,1]{1,0,4,3,2:T(8,128)(2,1)} %bitcast.575, bf16[4,8,7,7,512]{4,3,2,1,0:T(8,128)(2,1)S(1)} %dot_general.77), kind=kOutput, calls=%fused_computation.155 | convolution fusion | flops 7398752256 | bytes 35225600 | tf_op jit(solution)/shard_map/dot_general | solution.py:33
  525.5 19.1 %fusion.65 = (f32[4,8,7,7,512]{4,1,3,2,0:T(8,128)}, f32[4,8,7,7,512]{4,1,3,2,0:T(8,128)S(1)}, f32[4,8,7,7,512]{4,1,3,2,0:T(8,128)}, f32[4,8,7,7,512]{4,1,3,2,0:T...) fusion(f32[4,8,7,7,4608]{4,1,3,2,0:T(8,128)} %fusion.19), kind=kLoop, calls=%fused_computation.493 | loop fusion | bytes 57802752 | tf_op jit(solution)/shard_map/transpose(jvp())/split | solution.py:141
  544.7 5.3 pad_add_fusion.2
  550.3 4.4 pad_add_fusion.15
  554.7 3.7 copy.372
  558.4 5.0 reshape.518
  563.5 3.8 fusion.56
  575.5 14.2 %convolution_convert_fusion.3 = bf16[9,512,512]{2,1,0:T(8,128)(2,1)} fusion(bf16[9,512,1568]{2,1,0:T(8,128)(2,1)} %bitcast.562, bf16[1568,512]{1,0:T(8,128)(2,1)S(1)} %copy-done.33), kind=kOutput, calls=%fused_computation.118 | convolution fusion | flops 7401111552 | bytes 20774912 | tf_op jit(solution)/shard_map/dot_general | solution.py:27
  601.8 7.0 convolution_convert_fusion.1
  608.8 17.6 %fusion.2 = (bf16[1568,2048]{1,0:T(8,128)(2,1)}, f32[1568,2048]{1,0:T(8,128)}) fusion(f32[1568,2048]{1,0:T(8,128)} %copy-done.2, bf16[1568,2048]{1,0:T(8,128)(2,1)} %param.24, f32[1568,2048]{1,0:T(8,128)} %get-tuple-element.196, bf16[1568,512]{1,0:T(8,128)(2,1)} %multiply_convert_fusion.3, bf16[2048,512]{1,0:T(8,128)(2,1)S(1)} %bitcast.566), kind=kOutput, calls=%fused_computation.20 | convolution fusion | flops 3310813184 | bytes 55083008 | tf_op jit(solution)/shard_map/dot_general | solution.py:33
  629.8 9.9 %dot_general.80 = bf16[4,8,7,7,2048]{4,3,2,1,0:T(8,128)(2,1)} reshape(bf16[1568,2048]{1,0:T(8,128)(2,1)} %get-tuple-element.370) | data formatting | bytes 12845056 | tf_op jit(solution)/shard_map/dot_general | solution.py:33
  639.7 30.8 %multiply_reduce_fusion.12 = (f32[512]{0:T(512)S(1)}, f32[512]{0:T(512)S(1)}, f32[512]{0:T(512)S(1)}, f32[512]{0:T(512)S(1)}, f32[512]{0:T(512)S(1)}, /*index=5*...) fusion(f32[4,8,7,7,512]{4,3,2,1,0:T(8,128)} %copy-done.17, ...), kind=kOutput, calls=%fused_computation.73 | convolution fusion | flops 3309989376 | bytes 40732672 | tf_op jit(solution)/shard_map/dot_general | solution.py:33
  670.8 4.5 broadcast_multiply_fusion
  675.3 10.2 %pad_add_fusion.1 = f32[4,8,9,9,512]{4,3,2,1,0:T(8,128)} fusion(f32[4,8,7,7,512]{4,3,2,1,0:T(8,128)} %get-tuple-element.233, f32[4,8,7,7,512]{4,3,2,1,0:T(8,128)} %get-tuple-element.234, f32[4,8,7,7,512]{4,3,2,1,0:T(8,128)} %broadcast_multiply_fusion), kind=kLoop, calls=%fused_computation.40 | loop fusion | flops 2654208 | bytes 14942208 | tf_op jit(solution)/shard_map/transpose(jvp())/add_any | solution.py:122
  685.6 13.6 %multiply_reduce_fusion.21 = (f32[512]{0:T(512)S(1)}, f32[512]{0:T(512)S(1)}, f32[512]{0:T(512)S(1)}, f32[512]{0:T(512)S(1)}, f32[512]{0:T(512)S(1)}, /*index=5*...) fusion(f32[4,8,7,7,512]{4,3,2,1,0:T(8,128)S(1)} %copy-done.8, ...), kind=kLoop, calls=%fused_computation.82 | loop fusion | flops 20868608 | bytes 35006464 | tf_op jit(solution)/shard_map/transpose(jvp())/reduce_sum | solution.py:122
  701.8 12.5 %broadcast_multiply_fusion.9 = (f32[4,8,7,7,512]{4,3,2,1,0:T(8,128)}, f32[4,8,7,7,512]{4,3,2,1,0:T(8,128)}, f32[4,8,7,7,512]{4,3,2,1,0:T(8,128)}, f32[4,8,7,7,51...) fusion(f32[4,8,7,7,512]{4,3,2,1,0:T(8,128)} %get-tuple-element., ...), kind=kLoop, calls=%fused_computation.145 | loop fusion | flops 7225344 | bytes 32131072 | tf_op jit(solution)/shard_map/transpose(jvp())/mul | solution.py:122
  714.3 6.4 pad_add_fusion
  720.8 7.5 pad_add_fusion.9
  730.7 8.8 fusion.10
  739.4 13.6 %add_convert_fusion = bf16[1568,2048]{1,0:T(8,128)(2,1)} fusion(f32[1568,2048]{1,0:T(8,128)} %get-tuple-element.371, f32[1568,2048]{1,0:T(8,128)} %copy-done.2, bf16[1568,512]{1,0:T(8,128)(2,1)} %convert_element_type.318, bf16[2048,512]{1,0:T(8,128)(2,1)S(1)} %bitcast.564), kind=kOutput, calls=%fused_computation.22 | convolution fusion | flops 3301179392 | bytes 35815424 | tf_op jit(solution)/shard_map/dot_general | solution.py:33
  756.1 7.4 fusion.15
  772.2 6.1 collective-permute-done.118
  778.4 3.8 collective-permute-done.80
  787.2 4.2 collective-permute-done.120
  792.3 3.7 collective-permute-done.81
  821.2 6.2 collective-permute-done.111
  829.0 9.5 collective-permute-done.97
  840.2 9.6 collective-permute-done.90
  851.5 8.6 collective-permute-done.83
  889.8 26.9 %collective-permute-done.104 = bf16[9,2,2,2,16,512]{5,4,3,2,1,0:T(8,128)(2,1)S(1)} collective-permute-done((bf16[9,2,2,2,16,512]{5,4,3,2,1,0:T(8,128)(2,1)S(1)}, bf16[9,2,2,2,16,512]{5,4,3,2,1,0:T(8,128)(2,1)S(1)}, u32[]{:S(2)}, u32[]{:S(2)}) %collective-permute-start.104) | collective-permute-done | bytes 1179680 | tf_op jit(solution)/shard_map/ppermute | solution.py:48
  918.3 13.6 %collective-permute-done.105 = bf16[9,2,2,16,512]{4,3,2,1,0:T(8,128)(2,1)S(1)} collective-permute-done((bf16[9,2,2,16,512]{4,3,2,1,0:T(8,128)(2,1)S(1)}, bf16[9,2,2,16,512]{4,3,2,1,0:T(8,128)(2,1)S(1)}, u32[]{:S(2)}, u32[]{:S(2)}) %collective-permute-start.105) | collective-permute-done | bytes 589856 | tf_op jit(solution)/shard_map/ppermute | solution.py:48
  933.0 6.8 collective-permute-done.106
  940.2 7.3 collective-permute-done.107
  948.1 4.7 collective-permute-done.108
  (900 shorter events, 358.4 us)
Async XLA Ops:
  1.7 44.5 %collective-permute-start.49 = (bf16[64,174]{1,0:T(8,128)(2,1)S(1)}, bf16[64,174]{1,0:T(8,128)(2,1)}, u32[]{:S(2)}, u32[]{:S(2)}) collective-permute-start(bf16[64,174]{1,0:T(8,128)(2,1)S(1)} %copy.406), channel_id=1, source_target_pairs={{0,16},{1,17},{2,18},{3,19},{4,20},{5,21},{6,22},{7,23},{8,24},{9,... | collective-permute-start | bytes 66824 | tf_op jit(solution)/shard_map/ppermute | solution.py:48
  7.3 46.9 %collective-permute-start.37 = (bf16[16,2048]{1,0:T(8,128)(2,1)}, bf16[16,2048]{1,0:T(8,128)(2,1)}, u32[]{:S(2)}, u32[]{:S(2)}) collective-permute-start(bf16[16,2048]{1,0:T(8,128)(2,1)} %constant_dynamic-slice_fusion.3), channel_id=1, source_target_pairs={{0,16},{1,17},{2,18},{3,19},{4,20},{5,21},{6,22},{7,23},{8,24},{9,... | collective-permute-start | bytes 196616 | tf_op jit(solution)/shard_map/ppermute | solution.py:48
  8.8 50.9 %collective-permute-start.13 = (bf16[64,512]{1,0:T(8,128)(2,1)}, bf16[64,512]{1,0:T(8,128)(2,1)}, u32[]{:S(2)}, u32[]{:S(2)}) collective-permute-start(bf16[64,512]{1,0:T(8,128)(2,1)} %constant_dynamic-slice_fusion.5), channel_id=1, source_target_pairs={{0,16},{1,17},{2,18},{3,19},{4,20},{5,21},{6,22},{7,23},{8,24},{9,... | collective-permute-start | bytes 196616 | tf_op jit(solution)/shard_map/ppermute | solution.py:48
  13.2 49.5 %collective-permute-start.8 = (bf16[128,256]{1,0:T(8,128)(2,1)}, bf16[128,256]{1,0:T(8,128)(2,1)}, u32[]{:S(2)}, u32[]{:S(2)}) collective-permute-start(bf16[128,256]{1,0:T(8,128)(2,1)} %constant_dynamic-slice_fusion.6), channel_id=1, source_target_pairs={{0,16},{1,17},{2,18},{3,19},{4,20},{5,21},{6,22},{7,23},{8,24},{9,... | collective-permute-start | bytes 196616 | tf_op jit(solution)/shard_map/ppermute | solution.py:48
  21.8 24.3 %collective-permute-start.5 = (bf16[56,128]{1,0:T(8,128)(2,1)}, bf16[56,128]{1,0:T(8,128)(2,1)S(1)}, u32[]{:S(2)}, u32[]{:S(2)}) collective-permute-start(bf16[56,128]{1,0:T(8,128)(2,1)} %pad_bitcast_fusion.1), channel_id=1, source_target_pairs={{0,16},{1,17},{2,18},{3,19},{4,20},{5,21},{6,22},{7,23},{8,24},{9,... | collective-permute-start | bytes 43016 | tf_op jit(solution)/shard_map/ppermute | solution.py:48
  46.2 10.4 %collective-permute-start = (bf16[64,512]{1,0:T(8,128)(2,1)}, bf16[64,512]{1,0:T(8,128)(2,1)S(1)}, u32[]{:S(2)}, u32[]{:S(2)}) collective-permute-start(bf16[64,512]{1,0:T(8,128)(2,1)} %constant_dynamic-slice_fusion.7), channel_id=1, source_target_pairs={{0,16},{1,17},{2,18},{3,19},{4,20},{5,21},{6,22},{7,23},{8,24},{9,... | collective-permute-start | bytes 196616 | tf_op jit(solution)/shard_map/ppermute | solution.py:48
  50.2 68.1 %collective-permute-start.25 = (bf16[9,16,512]{2,1,0:T(8,128)(2,1)}, bf16[9,16,512]{2,1,0:T(8,128)(2,1)}, u32[]{:S(2)}, u32[]{:S(2)}) collective-permute-start(bf16[9,16,512]{2,1,0:T(8,128)(2,1)} %constant_dynamic-slice_fusion.4), channel_id=1, source_target_pairs={{0,16},{1,17},{2,18},{3,19},{4,20},{5,21},{6,22},{7,23},{8,24},{9,... | collective-permute-start | bytes 442376 | tf_op jit(solution)/shard_map/ppermute | solution.py:48
  54.2 10.8 %collective-permute-start.50 = (bf16[2,64,174]{2,1,0:T(8,128)(2,1)S(1)}, bf16[2,64,174]{2,1,0:T(8,128)(2,1)S(1)}, u32[]{:S(2)}, u32[]{:S(2)}) collective-permute-start(bf16[2,64,174]{2,1,0:T(8,128)(2,1)S(1)} %pad_maximum_fusion.42), channel_id=1, source_target_pairs={{0,8},{1,9},{2,10},{3,11},{4,12},{5,13},{6,14},{7,15},{8,0},{9,1},... | collective-permute-start | bytes 133640 | tf_op jit(solution)/shard_map/ppermute | solution.py:48
  56.6 10.6 %collective-permute-start.7 = (bf16[2,2,56,128]{3,2,1,0:T(8,128)(2,1)S(1)}, bf16[2,2,56,128]{3,2,1,0:T(8,128)(2,1)S(1)}, u32[]{:S(2)}, u32[]{:S(2)}) collective-permute-start(bf16[2,2,56,128]{3,2,1,0:T(8,128)(2,1)S(1)} %pad_maximum_fusion.44), channel_id=1, source_target_pairs={{0,4},{1,5},{2,6},{3,7},{4,0},{5,1},{6,2},{7,3},{8,12},{9,13},{10,... | collective-permute-start | bytes 172040 | tf_op jit(solution)/shard_map/ppermute | solution.py:48
  59.7 66.1 %collective-permute-start.38 = (bf16[2,16,2048]{2,1,0:T(8,128)(2,1)}, bf16[2,16,2048]{2,1,0:T(8,128)(2,1)}, u32[]{:S(2)}, u32[]{:S(2)}) collective-permute-start(bf16[2,16,2048]{2,1,0:T(8,128)(2,1)} %pad_maximum_fusion.35), channel_id=1, source_target_pairs={{0,8},{1,9},{2,10},{3,11},{4,12},{5,13},{6,14},{7,15},{8,0},{9,1},... | collective-permute-start | bytes 393224 | tf_op jit(solution)/shard_map/ppermute | solution.py:48
  62.7 66.0 %collective-permute-start.14 = (bf16[2,64,512]{2,1,0:T(8,128)(2,1)}, bf16[2,64,512]{2,1,0:T(8,128)(2,1)}, u32[]{:S(2)}, u32[]{:S(2)}) collective-permute-start(bf16[2,64,512]{2,1,0:T(8,128)(2,1)} %pad_maximum_fusion.34), channel_id=1, source_target_pairs={{0,8},{1,9},{2,10},{3,11},{4,12},{5,13},{6,14},{7,15},{8,0},{9,1},... | collective-permute-start | bytes 393224 | tf_op jit(solution)/shard_map/ppermute | solution.py:48
  65.0 65.2 %collective-permute-start.9 = (bf16[2,128,256]{2,1,0:T(8,128)(2,1)}, bf16[2,128,256]{2,1,0:T(8,128)(2,1)}, u32[]{:S(2)}, u32[]{:S(2)}) collective-permute-start(bf16[2,128,256]{2,1,0:T(8,128)(2,1)} %pad_maximum_fusion.33), channel_id=1, source_target_pairs={{0,8},{1,9},{2,10},{3,11},{4,12},{5,13},{6,14},{7,15},{8,0},{9,1},... | collective-permute-start | bytes 393224 | tf_op jit(solution)/shard_map/ppermute | solution.py:48
  67.2 65.7 %collective-permute-start.1 = (bf16[2,64,512]{2,1,0:T(8,128)(2,1)}, bf16[2,64,512]{2,1,0:T(8,128)(2,1)}, u32[]{:S(2)}, u32[]{:S(2)}) collective-permute-start(bf16[2,64,512]{2,1,0:T(8,128)(2,1)} %pad_maximum_fusion.32), channel_id=1, source_target_pairs={{0,8},{1,9},{2,10},{3,11},{4,12},{5,13},{6,14},{7,15},{8,0},{9,1},... | collective-permute-start | bytes 393224 | tf_op jit(solution)/shard_map/ppermute | solution.py:48
  123.8 13.2 %collective-permute-start.26 = (bf16[9,2,16,512]{3,2,0,1:T(8,128)(2,1)S(1)}, bf16[9,2,16,512]{3,2,0,1:T(8,128)(2,1)S(1)}, u32[]{:S(2)}, u32[]{:S(2)}) collective-permute-start(bf16[9,2,16,512]{3,2,0,1:T(8,128)(2,1)S(1)} %pad_maximum_fusion.22), channel_id=1, source_target_pairs={{0,8},{1,9},{2,10},{3,11},{4,12},{5,13},{6,14},{7,15},{8,0},{9,1},... | collective-permute-start | bytes 884744 | tf_op jit(solution)/shard_map/ppermute | solution.py:48
  128.7 9.4 collective-permute-start.39
  130.2 9.9 %collective-permute-start.15 = (bf16[2,2,64,512]{3,2,1,0:T(8,128)(2,1)S(1)}, bf16[2,2,64,512]{3,2,1,0:T(8,128)(2,1)S(1)}, u32[]{:S(2)}, u32[]{:S(2)}) collective-permute-start(bf16[2,2,64,512]{3,2,1,0:T(8,128)(2,1)S(1)} %pad_maximum_fusion.26), channel_id=1, source_target_pairs={{0,4},{1,5},{2,6},{3,7},{4,0},{5,1},{6,2},{7,3},{8,12},{9,13},{10,... | collective-permute-start | bytes 786440 | tf_op jit(solution)/shard_map/ppermute | solution.py:48
  132.8 11.6 %collective-permute-start.10 = (bf16[2,2,128,256]{3,2,1,0:T(8,128)(2,1)S(1)}, bf16[2,2,128,256]{3,2,1,0:T(8,128)(2,1)S(1)}, u32[]{:S(2)}, u32[]{:S(2)}) collective-permute-start(bf16[2,2,128,256]{3,2,1,0:T(8,128)(2,1)S(1)} %pad_maximum_fusion.25), channel_id=1, source_target_pairs={{0,4},{1,5},{2,6},{3,7},{4,0},{5,1},{6,2},{7,3},{8,12},{9,13},{10,... | collective-permute-start | bytes 786440 | tf_op jit(solution)/shard_map/ppermute | solution.py:48
  134.4 15.7 %collective-permute-start.2 = (bf16[2,2,64,512]{3,2,1,0:T(8,128)(2,1)S(1)}, bf16[2,2,64,512]{3,2,1,0:T(8,128)(2,1)S(1)}, u32[]{:S(2)}, u32[]{:S(2)}) collective-permute-start(bf16[2,2,64,512]{3,2,1,0:T(8,128)(2,1)S(1)} %pad_maximum_fusion.24), channel_id=1, source_target_pairs={{0,4},{1,5},{2,6},{3,7},{4,0},{5,1},{6,2},{7,3},{8,12},{9,13},{10,... | collective-permute-start | bytes 786440 | tf_op jit(solution)/shard_map/ppermute | solution.py:48
  137.0 211.7 %collective-permute-start.53 = (bf16[2,2,2,2,64,174]{5,4,3,2,1,0:T(8,128)(2,1)}, bf16[2,2,2,2,64,174]{5,4,3,2,1,0:T(8,128)(2,1)}, u32[]{:S(2)}, u32[]{:S(2)}) collective-permute-start(bf16[2,2,2,2,64,174]{5,4,3,2,1,0:T(8,128)(2,1)} %pad_maximum_fusion.21), channel_id=1, source_target_pairs={{0,1},{1,0},{2,3},{3,2},{4,5},{5,4},{6,7},{7,6},{8,9},{9,8},{10,11... | collective-permute-start | bytes 1069064 | tf_op jit(solution)/shard_map/ppermute | solution.py:48
  138.1 98.6 %collective-permute-start.27 = (bf16[9,2,2,16,512]{4,3,0,1,2:T(8,128)(2,1)}, bf16[9,2,2,16,512]{4,3,0,1,2:T(8,128)(2,1)}, u32[]{:S(2)}, u32[]{:S(2)}) collective-permute-start(bf16[9,2,2,16,512]{4,3,0,1,2:T(8,128)(2,1)} %pad_maximum_fusion.15), channel_id=1, source_target_pairs={{0,4},{1,5},{2,6},{3,7},{4,0},{5,1},{6,2},{7,3},{8,12},{9,13},{10,... | collective-permute-start | bytes 1769480 | tf_op jit(solution)/shard_map/ppermute | solution.py:48
  140.1 46.6 %collective-permute-start.40 = (bf16[2,2,2,16,2048]{4,3,2,1,0:T(8,128)(2,1)S(1)}, bf16[2,2,2,16,2048]{4,3,2,1,0:T(8,128)(2,1)S(1)}, u32[]{:S(2)}, u32[]{:S(2)}) collective-permute-start(bf16[2,2,2,16,2048]{4,3,2,1,0:T(8,128)(2,1)S(1)} %pad_maximum_fusion.20), channel_id=1, source_target_pairs={{0,2},{1,3},{2,0},{3,1},{4,6},{5,7},{6,4},{7,5},{8,10},{9,11},{10,... | collective-permute-start | bytes 1572872 | tf_op jit(solution)/shard_map/ppermute | solution.py:48
  144.4 21.8 %collective-permute-start.16 = (bf16[2,2,2,64,512]{4,3,2,1,0:T(8,128)(2,1)S(1)}, bf16[2,2,2,64,512]{4,3,2,1,0:T(8,128)(2,1)S(1)}, u32[]{:S(2)}, u32[]{:S(2)}) collective-permute-start(bf16[2,2,2,64,512]{4,3,2,1,0:T(8,128)(2,1)S(1)} %pad_maximum_fusion.19), channel_id=1, source_target_pairs={{0,2},{1,3},{2,0},{3,1},{4,6},{5,7},{6,4},{7,5},{8,10},{9,11},{10,... | collective-permute-start | bytes 1572872 | tf_op jit(solution)/shard_map/ppermute | solution.py:48
  150.0 27.4 %collective-permute-start.11 = (bf16[2,2,2,128,256]{4,3,2,1,0:T(8,128)(2,1)S(1)}, bf16[2,2,2,128,256]{4,3,2,1,0:T(8,128)(2,1)S(1)}, u32[]{:S(2)}, u32[]{:S(2)}) collective-permute-start(bf16[2,2,2,128,256]{4,3,2,1,0:T(8,128)(2,1)S(1)} %pad_maximum_fusion.18), channel_id=1, source_target_pairs={{0,2},{1,3},{2,0},{3,1},{4,6},{5,7},{6,4},{7,5},{8,10},{9,11},{10,... | collective-permute-start | bytes 1572872 | tf_op jit(solution)/shard_map/ppermute | solution.py:48
  166.2 20.3 %collective-permute-start.3 = (bf16[2,2,2,64,512]{4,3,2,1,0:T(8,128)(2,1)S(1)}, bf16[2,2,2,64,512]{4,3,2,1,0:T(8,128)(2,1)S(1)}, u32[]{:S(2)}, u32[]{:S(2)}) collective-permute-start(bf16[2,2,2,64,512]{4,3,2,1,0:T(8,128)(2,1)S(1)} %pad_maximum_fusion.17), channel_id=1, source_target_pairs={{0,2},{1,3},{2,0},{3,1},{4,6},{5,7},{6,4},{7,5},{8,10},{9,11},{10,... | collective-permute-start | bytes 1572872 | tf_op jit(solution)/shard_map/ppermute | solution.py:48
  177.5 11.8 %collective-permute-start.17 = (bf16[2,2,2,2,64,512]{5,4,3,2,1,0:T(8,128)(2,1)S(1)}, bf16[2,2,2,2,64,512]{5,4,3,2,1,0:T(8,128)(2,1)S(1)}, u32[]{:S(2)}, u32[]{:S(2)}) collective-permute-start(bf16[2,2,2,2,64,512]{5,4,3,2,1,0:T(8,128)(2,1)S(1)} %pad_maximum_fusion.10), channel_id=1, source_target_pairs={{0,1},{1,0},{2,3},{3,2},{4,5},{5,4},{6,7},{7,6},{8,9},{9,8},{10,11... | collective-permute-start | bytes 3145736 | tf_op jit(solution)/shard_map/ppermute | solution.py:48
  189.2 56.2 %collective-permute-start.41 = (bf16[2,2,2,2,16,2048]{5,4,3,2,1,0:T(8,128)(2,1)}, bf16[2,2,2,2,16,2048]{5,4,3,2,1,0:T(8,128)(2,1)}, u32[]{:S(2)}, u32[]{:S(2)}) collective-permute-start(bf16[2,2,2,2,16,2048]{5,4,3,2,1,0:T(8,128)(2,1)} %pad_maximum_fusion.11), channel_id=1, source_target_pairs={{0,1},{1,0},{2,3},{3,2},{4,5},{5,4},{6,7},{7,6},{8,9},{9,8},{10,11... | collective-permute-start | bytes 3145736 | tf_op jit(solution)/shard_map/ppermute | solution.py:48
  242.6 58.5 %collective-permute-start.28 = (bf16[9,2,2,2,16,512]{5,4,0,1,2,3:T(8,128)(2,1)}, bf16[9,2,2,2,16,512]{5,4,0,1,2,3:T(8,128)(2,1)}, u32[]{:S(2)}, u32[]{:S(2)}) collective-permute-start(bf16[9,2,2,2,16,512]{5,4,0,1,2,3:T(8,128)(2,1)} %pad_maximum_fusion.7), channel_id=1, source_target_pairs={{0,2},{1,3},{2,0},{3,1},{4,6},{5,7},{6,4},{7,5},{8,10},{9,11},{10,... | collective-permute-start | bytes 3538952 | tf_op jit(solution)/shard_map/ppermute | solution.py:48
  380.4 34.4 %collective-permute-start.55 = (f32[4,174]{1,0:T(4,128)S(1)}, f32[4,174]{1,0:T(4,128)S(1)}, u32[]{:S(2)}, u32[]{:S(2)}) collective-permute-start(f32[4,174]{1,0:T(4,128)S(1)} %convolution_add_fusion.1), channel_id=1, source_target_pairs={{1,0},{2,1},{3,2},{4,3},{5,4},{6,5},{7,6},{8,7},{9,8},{10,9},{11,1... | collective-permute-start | bytes 8360 | tf_op jit(solution)/shard_map/ppermute | solution.py:323
  381.8 32.9 %collective-permute-start.54 = (f32[4,174]{1,0:T(4,128)S(1)}, f32[4,174]{1,0:T(4,128)S(1)}, u32[]{:S(2)}, u32[]{:S(2)}) collective-permute-start(f32[4,174]{1,0:T(4,128)S(1)} %convolution_add_fusion.1), channel_id=1, source_target_pairs={{0,1},{1,2},{2,3},{3,4},{4,5},{5,6},{6,7},{7,8},{8,9},{9,10},{10,1... | collective-permute-start | bytes 8360 | tf_op jit(solution)/shard_map/ppermute | solution.py:322
  437.2 9.4 collective-permute-start.59
  446.7 21.5 %collective-permute-start.62 = (f32[4271]{0:T(1024)S(1)}, f32[4271]{0:T(1024)S(1)}, u32[]{:S(2)}, u32[]{:S(2)}) collective-permute-start(f32[4271]{0:T(1024)S(1)} %add_add_fusion.2), channel_id=1, source_target_pairs={{0,24},{1,25},{2,26},{3,27},{4,28},{5,29},{6,30},{7,31},{8,16},{9,... | collective-permute-start | bytes 51260 | tf_op jit(solution)/shard_map/ppermute | solution.py:48
  449.0 19.2 %collective-permute-start.61 = (f32[4271]{0:T(1024)S(1)}, f32[4271]{0:T(1024)S(1)}, u32[]{:S(2)}, u32[]{:S(2)}) collective-permute-start(f32[4271]{0:T(1024)S(1)} %add_add_fusion.2), channel_id=1, source_target_pairs={{0,16},{1,17},{2,18},{3,19},{4,20},{5,21},{6,22},{7,23},{8,24},{9,... | collective-permute-start | bytes 51260 | tf_op jit(solution)/shard_map/ppermute | solution.py:48
  450.2 18.1 %collective-permute-start.60 = (f32[4271]{0:T(1024)S(1)}, f32[4271]{0:T(1024)S(1)}, u32[]{:S(2)}, u32[]{:S(2)}) collective-permute-start(f32[4271]{0:T(1024)S(1)} %add_add_fusion.2), channel_id=1, source_target_pairs={{0,8},{1,9},{2,10},{3,11},{4,12},{5,13},{6,14},{7,15},{8,0},{9,1},... | collective-permute-start | bytes 51260 | tf_op jit(solution)/shard_map/ppermute | solution.py:48
  491.4 275.4 %collective-permute-start.117 = (bf16[2,2,2,2,64,174]{5,4,3,2,1,0:T(8,128)(2,1)}, bf16[2,2,2,2,64,174]{5,4,3,2,1,0:T(8,128)(2,1)}, u32[]{:S(2)}, u32[]{:S(2)}) collective-permute-start(bf16[2,2,2,2,64,174]{5,4,3,2,1,0:T(8,128)(2,1)} %dynamic-slice_bitcast_fusion.7), channel_id=1, source_target_pairs={{0,1},{1,0},{2,3},{3,2},{4,5},{5,4},{6,7},{7,6},{8,9},{9,8},{10,11... | collective-permute-start | bytes 1069064 | tf_op jit(solution)/shard_map/ppermute | solution.py:48
  493.4 14.1 %collective-permute-start.69 = (f32[1024]{0:T(1024)S(1)}, f32[1024]{0:T(1024)S(1)}, u32[]{:S(2)}, u32[]{:S(2)}) collective-permute-start(f32[1024]{0:T(1024)S(1)} %add_add_fusion.10), channel_id=1, source_target_pairs={{0,24},{1,25},{2,26},{3,27},{4,28},{5,29},{6,30},{7,31},{8,16},{9,... | collective-permute-start | bytes 12296 | tf_op jit(solution)/shard_map/ppermute | solution.py:48
  495.7 11.8 %collective-permute-start.68 = (f32[1024]{0:T(1024)S(1)}, f32[1024]{0:T(1024)S(1)}, u32[]{:S(2)}, u32[]{:S(2)}) collective-permute-start(f32[1024]{0:T(1024)S(1)} %add_add_fusion.10), channel_id=1, source_target_pairs={{0,16},{1,17},{2,18},{3,19},{4,20},{5,21},{6,22},{7,23},{8,24},{9,... | collective-permute-start | bytes 12296 | tf_op jit(solution)/shard_map/ppermute | solution.py:48
  495.9 11.5 %collective-permute-start.67 = (f32[1024]{0:T(1024)S(1)}, f32[1024]{0:T(1024)S(1)}, u32[]{:S(2)}, u32[]{:S(2)}) collective-permute-start(f32[1024]{0:T(1024)S(1)} %add_add_fusion.10), channel_id=1, source_target_pairs={{0,8},{1,9},{2,10},{3,11},{4,12},{5,13},{6,14},{7,15},{8,0},{9,1},... | collective-permute-start | bytes 12296 | tf_op jit(solution)/shard_map/ppermute | solution.py:48
  570.8 239.8 %collective-permute-start.110 = (bf16[2,2,2,2,16,2048]{5,4,3,2,1,0:T(8,128)(2,1)}, bf16[2,2,2,2,16,2048]{5,4,3,2,1,0:T(8,128)(2,1)}, u32[]{:S(2)}, u32[]{:S(2)}) collective-permute-start(bf16[2,2,2,2,16,2048]{5,4,3,2,1,0:T(8,128)(2,1)} %dynamic-slice_bitcast_fusion.2), channel_id=1, source_target_pairs={{0,1},{1,0},{2,3},{3,2},{4,5},{5,4},{6,7},{7,6},{8,9},{9,8},{10,11... | collective-permute-start | bytes 3145736 | tf_op jit(solution)/shard_map/ppermute | solution.py:48
  572.0 17.8 %collective-permute-start.73 = (f32[1024]{0:T(1024)S(1)}, f32[1024]{0:T(1024)S(1)}, u32[]{:S(2)}, u32[]{:S(2)}) collective-permute-start(f32[1024]{0:T(1024)S(1)} %fusion.46), channel_id=1, source_target_pairs={{0,6},{1,7},{2,4},{3,5},{4,2},{5,3},{6,0},{7,1},{8,14},{9,15},{10,... | collective-permute-start | bytes 12296 | tf_op jit(solution)/shard_map/ppermute | solution.py:48
  573.8 15.9 %collective-permute-start.72 = (f32[1024]{0:T(1024)S(1)}, f32[1024]{0:T(1024)S(1)}, u32[]{:S(2)}, u32[]{:S(2)}) collective-permute-start(f32[1024]{0:T(1024)S(1)} %fusion.46), channel_id=1, source_target_pairs={{0,4},{1,5},{2,6},{3,7},{4,0},{5,1},{6,2},{7,3},{8,12},{9,13},{10,... | collective-permute-start | bytes 12296 | tf_op jit(solution)/shard_map/ppermute | solution.py:48
  574.4 15.4 %collective-permute-start.71 = (f32[1024]{0:T(1024)S(1)}, f32[1024]{0:T(1024)S(1)}, u32[]{:S(2)}, u32[]{:S(2)}) collective-permute-start(f32[1024]{0:T(1024)S(1)} %fusion.46), channel_id=1, source_target_pairs={{0,2},{1,3},{2,0},{3,1},{4,6},{5,7},{6,4},{7,5},{8,10},{9,11},{10,... | collective-permute-start | bytes 12296 | tf_op jit(solution)/shard_map/ppermute | solution.py:48
  589.8 9.3 collective-permute-start.76
  599.1 287.0 %collective-permute-start.103 = (bf16[9,2,2,2,2,16,512]{6,5,4,3,2,1,0:T(8,128)(2,1)}, bf16[9,2,2,2,2,16,512]{6,5,4,3,2,1,0:T(8,128)(2,1)}, u32[]{:S(2)}, u32[]{:S(2)}) collective-permute-start(bf16[9,2,2,2,2,16,512]{6,5,4,3,2,1,0:T(8,128)(2,1)} %dynamic-slice_bitcast_fusion), channel_id=1, source_target_pairs={{0,1},{1,0},{2,3},{3,2},{4,5},{5,4},{6,7},{7,6},{8,9},{9,8},{10,11... | collective-permute-start | bytes 7077896 | tf_op jit(solution)/shard_map/ppermute | solution.py:48
  629.2 184.6 %collective-permute-start.96 = (bf16[2,2,2,2,64,512]{5,4,3,2,1,0:T(8,128)(2,1)}, bf16[2,2,2,2,64,512]{5,4,3,2,1,0:T(8,128)(2,1)}, u32[]{:S(2)}, u32[]{:S(2)}) collective-permute-start(bf16[2,2,2,2,64,512]{5,4,3,2,1,0:T(8,128)(2,1)} %dynamic-slice_bitcast_fusion.3), channel_id=1, source_target_pairs={{0,1},{1,0},{2,3},{3,2},{4,5},{5,4},{6,7},{7,6},{8,9},{9,8},{10,11... | collective-permute-start | bytes 3145736 | tf_op jit(solution)/shard_map/ppermute | solution.py:48
  700.9 62.7 %collective-permute-start.77 = (bf16[8,48,128]{2,1,0:T(8,128)(2,1)}, bf16[8,48,128]{2,1,0:T(8,128)(2,1)}, u32[]{:S(2)}, u32[]{:S(2)}) collective-permute-start(bf16[8,48,128]{2,1,0:T(8,128)(2,1)} %copy.379), channel_id=1, source_target_pairs={{0,2},{1,3},{2,0},{3,1},{4,6},{5,7},{6,4},{7,5},{8,10},{9,11},{10,... | collective-permute-start | bytes 294920 | tf_op jit(solution)/shard_map/ppermute | solution.py:48
  766.5 49.6 %collective-permute-start.89 = (bf16[2,2,2,2,128,256]{5,4,3,2,1,0:T(8,128)(2,1)S(1)}, bf16[2,2,2,2,128,256]{5,4,3,2,1,0:T(8,128)(2,1)}, u32[]{:S(2)}, u32[]{:S(2)}) collective-permute-start(bf16[2,2,2,2,128,256]{5,4,3,2,1,0:T(8,128)(2,1)S(1)} %dynamic-slice_bitcast_fusion.4), channel_id=1, source_target_pairs={{0,1},{1,0},{2,3},{3,2},{4,5},{5,4},{6,7},{7,6},{8,9},{9,8},{10,11... | collective-permute-start | bytes 3145736 | tf_op jit(solution)/shard_map/ppermute | solution.py:48
  808.4 10.5 %collective-permute-start.82 = (bf16[2,2,2,2,64,512]{5,4,3,2,1,0:T(8,128)(2,1)}, bf16[2,2,2,2,64,512]{5,4,3,2,1,0:T(8,128)(2,1)}, u32[]{:S(2)}, u32[]{:S(2)}) collective-permute-start(bf16[2,2,2,2,64,512]{5,4,3,2,1,0:T(8,128)(2,1)} %dynamic-slice_bitcast_fusion.5), channel_id=1, source_target_pairs={{0,1},{1,0},{2,3},{3,2},{4,5},{5,4},{6,7},{7,6},{8,9},{9,8},{10,11... | collective-permute-start | bytes 3145736 | tf_op jit(solution)/shard_map/ppermute | solution.py:48
  812.5 14.9 %collective-permute-start.111 = (bf16[2,2,2,16,2048]{4,3,2,1,0:T(8,128)(2,1)S(1)}, bf16[2,2,2,16,2048]{4,3,2,1,0:T(8,128)(2,1)S(1)}, u32[]{:S(2)}, u32[]{:S(2)}) collective-permute-start(bf16[2,2,2,16,2048]{4,3,2,1,0:T(8,128)(2,1)S(1)} %dynamic-slice_bitcast_fusion.8), channel_id=1, source_target_pairs={{0,2},{1,3},{2,0},{3,1},{4,6},{5,7},{6,4},{7,5},{8,10},{9,11},{10,... | collective-permute-start | bytes 1572872 | tf_op jit(solution)/shard_map/ppermute | solution.py:48
  815.3 23.3 %collective-permute-start.97 = (bf16[2,2,2,64,512]{4,3,2,1,0:T(8,128)(2,1)S(1)}, bf16[2,2,2,64,512]{4,3,2,1,0:T(8,128)(2,1)S(1)}, u32[]{:S(2)}, u32[]{:S(2)}) collective-permute-start(bf16[2,2,2,64,512]{4,3,2,1,0:T(8,128)(2,1)S(1)} %dynamic-slice_bitcast_fusion.9), channel_id=1, source_target_pairs={{0,2},{1,3},{2,0},{3,1},{4,6},{5,7},{6,4},{7,5},{8,10},{9,11},{10,... | collective-permute-start | bytes 1572872 | tf_op jit(solution)/shard_map/ppermute | solution.py:48
  817.5 32.2 %collective-permute-start.90 = (bf16[2,2,2,128,256]{4,3,2,1,0:T(8,128)(2,1)S(1)}, bf16[2,2,2,128,256]{4,3,2,1,0:T(8,128)(2,1)S(1)}, u32[]{:S(2)}, u32[]{:S(2)}) collective-permute-start(bf16[2,2,2,128,256]{4,3,2,1,0:T(8,128)(2,1)S(1)} %dynamic-slice_bitcast_fusion.10), channel_id=1, source_target_pairs={{0,2},{1,3},{2,0},{3,1},{4,6},{5,7},{6,4},{7,5},{8,10},{9,11},{10,... | collective-permute-start | bytes 1572872 | tf_op jit(solution)/shard_map/ppermute | solution.py:48
  820.4 39.7 %collective-permute-start.83 = (bf16[2,2,2,64,512]{4,3,2,1,0:T(8,128)(2,1)S(1)}, bf16[2,2,2,64,512]{4,3,2,1,0:T(8,128)(2,1)S(1)}, u32[]{:S(2)}, u32[]{:S(2)}) collective-permute-start(bf16[2,2,2,64,512]{4,3,2,1,0:T(8,128)(2,1)S(1)} %dynamic-slice_bitcast_fusion.11), channel_id=1, source_target_pairs={{0,2},{1,3},{2,0},{3,1},{4,6},{5,7},{6,4},{7,5},{8,10},{9,11},{10,... | collective-permute-start | bytes 1572872 | tf_op jit(solution)/shard_map/ppermute | solution.py:48
  827.4 34.3 %collective-permute-start.112 = (bf16[2,2,16,2048]{3,2,1,0:T(8,128)(2,1)S(1)}, bf16[2,2,16,2048]{3,2,1,0:T(8,128)(2,1)S(1)}, u32[]{:S(2)}, u32[]{:S(2)}) collective-permute-start(bf16[2,2,16,2048]{3,2,1,0:T(8,128)(2,1)S(1)} %dynamic-slice_bitcast_fusion.14), channel_id=1, source_target_pairs={{0,4},{1,5},{2,6},{3,7},{4,0},{5,1},{6,2},{7,3},{8,12},{9,13},{10,... | collective-permute-start | bytes 786440 | tf_op jit(solution)/shard_map/ppermute | solution.py:48
  838.6 23.2 %collective-permute-start.98 = (bf16[2,2,64,512]{3,2,1,0:T(8,128)(2,1)S(1)}, bf16[2,2,64,512]{3,2,1,0:T(8,128)(2,1)S(1)}, u32[]{:S(2)}, u32[]{:S(2)}) collective-permute-start(bf16[2,2,64,512]{3,2,1,0:T(8,128)(2,1)S(1)} %dynamic-slice_bitcast_fusion.15), channel_id=1, source_target_pairs={{0,4},{1,5},{2,6},{3,7},{4,0},{5,1},{6,2},{7,3},{8,12},{9,13},{10,... | collective-permute-start | bytes 786440 | tf_op jit(solution)/shard_map/ppermute | solution.py:48
  849.9 14.2 %collective-permute-start.91 = (bf16[2,2,128,256]{3,2,1,0:T(8,128)(2,1)S(1)}, bf16[2,2,128,256]{3,2,1,0:T(8,128)(2,1)S(1)}, u32[]{:S(2)}, u32[]{:S(2)}) collective-permute-start(bf16[2,2,128,256]{3,2,1,0:T(8,128)(2,1)S(1)} %dynamic-slice_bitcast_fusion.16), channel_id=1, source_target_pairs={{0,4},{1,5},{2,6},{3,7},{4,0},{5,1},{6,2},{7,3},{8,12},{9,13},{10,... | collective-permute-start | bytes 786440 | tf_op jit(solution)/shard_map/ppermute | solution.py:48
  862.0 9.9 %collective-permute-start.99 = (bf16[2,64,512]{2,1,0:T(8,128)(2,1)S(1)}, bf16[2,64,512]{2,1,0:T(8,128)(2,1)S(1)}, u32[]{:S(2)}, u32[]{:S(2)}) collective-permute-start(bf16[2,64,512]{2,1,0:T(8,128)(2,1)S(1)} %dynamic-slice_bitcast_fusion.21), channel_id=1, source_target_pairs={{0,8},{1,9},{2,10},{3,11},{4,12},{5,13},{6,14},{7,15},{8,0},{9,1},... | collective-permute-start | bytes 393224 | tf_op jit(solution)/shard_map/ppermute | solution.py:48
  864.1 11.9 %collective-permute-start.92 = (bf16[2,128,256]{2,1,0:T(8,128)(2,1)S(1)}, bf16[2,128,256]{2,1,0:T(8,128)(2,1)S(1)}, u32[]{:S(2)}, u32[]{:S(2)}) collective-permute-start(bf16[2,128,256]{2,1,0:T(8,128)(2,1)S(1)} %dynamic-slice_bitcast_fusion.22), channel_id=1, source_target_pairs={{0,8},{1,9},{2,10},{3,11},{4,12},{5,13},{6,14},{7,15},{8,0},{9,1},... | collective-permute-start | bytes 393224 | tf_op jit(solution)/shard_map/ppermute | solution.py:48
  867.7 10.1 %collective-permute-start.85 = (bf16[2,64,512]{2,1,0:T(8,128)(2,1)S(1)}, bf16[2,64,512]{2,1,0:T(8,128)(2,1)S(1)}, u32[]{:S(2)}, u32[]{:S(2)}) collective-permute-start(bf16[2,64,512]{2,1,0:T(8,128)(2,1)S(1)} %dynamic-slice_bitcast_fusion.23), channel_id=1, source_target_pairs={{0,8},{1,9},{2,10},{3,11},{4,12},{5,13},{6,14},{7,15},{8,0},{9,1},... | collective-permute-start | bytes 393224 | tf_op jit(solution)/shard_map/ppermute | solution.py:48
  868.4 10.8 %collective-permute-start.114 = (bf16[16,2048]{1,0:T(8,128)(2,1)S(1)}, bf16[16,2048]{1,0:T(8,128)(2,1)S(1)}, u32[]{:S(2)}, u32[]{:S(2)}) collective-permute-start(bf16[16,2048]{1,0:T(8,128)(2,1)S(1)} %dynamic-slice_bitcast_fusion.25), channel_id=1, source_target_pairs={{0,16},{1,17},{2,18},{3,19},{4,20},{5,21},{6,22},{7,23},{8,24},{9,... | collective-permute-start | bytes 196616 | tf_op jit(solution)/shard_map/ppermute | solution.py:48
  871.9 9.0 collective-permute-start.100
  886.0 32.3 %collective-permute-start.102 = (bf16[2,64,512]{2,1,0:T(8,128)(2,1)S(1)}, bf16[2,64,512]{2,1,0:T(8,128)(2,1)S(1)}, u32[]{:S(2)}, u32[]{:S(2)}) collective-permute-start(bf16[2,64,512]{2,1,0:T(8,128)(2,1)S(1)} %pad_maximum_fusion.39), channel_id=1, source_target_pairs={{0,1},{1,0},{2,3},{3,2},{4,5},{5,4},{6,7},{7,6},{8,9},{9,8},{10,11... | collective-permute-start | bytes 393224 | tf_op jit(solution)/shard_map/ppermute | solution.py:48
  888.3 28.4 %collective-permute-start.104 = (bf16[9,2,2,2,16,512]{5,4,3,2,1,0:T(8,128)(2,1)S(1)}, bf16[9,2,2,2,16,512]{5,4,3,2,1,0:T(8,128)(2,1)S(1)}, u32[]{:S(2)}, u32[]{:S(2)}) collective-permute-start(bf16[9,2,2,2,16,512]{5,4,3,2,1,0:T(8,128)(2,1)S(1)} %dynamic-slice_bitcast_fusion.1), channel_id=1, source_target_pairs={{0,2},{1,3},{2,0},{3,1},{4,6},{5,7},{6,4},{7,5},{8,10},{9,11},{10,... | collective-permute-start | bytes 3538952 | tf_op jit(solution)/shard_map/ppermute | solution.py:48
  889.1 51.2 %collective-permute-start.95 = (bf16[2,128,256]{2,1,0:T(8,128)(2,1)S(1)}, bf16[2,128,256]{2,1,0:T(8,128)(2,1)S(1)}, u32[]{:S(2)}, u32[]{:S(2)}) collective-permute-start(bf16[2,128,256]{2,1,0:T(8,128)(2,1)S(1)} %pad_maximum_fusion.38), channel_id=1, source_target_pairs={{0,1},{1,0},{2,3},{3,2},{4,5},{5,4},{6,7},{7,6},{8,9},{9,8},{10,11... | collective-permute-start | bytes 393224 | tf_op jit(solution)/shard_map/ppermute | solution.py:48
  889.4 58.7 %collective-permute-start.88 = (bf16[2,64,512]{2,1,0:T(8,128)(2,1)S(1)}, bf16[2,64,512]{2,1,0:T(8,128)(2,1)S(1)}, u32[]{:S(2)}, u32[]{:S(2)}) collective-permute-start(bf16[2,64,512]{2,1,0:T(8,128)(2,1)S(1)} %pad_maximum_fusion.37), channel_id=1, source_target_pairs={{0,1},{1,0},{2,3},{3,2},{4,5},{5,4},{6,7},{7,6},{8,9},{9,8},{10,11... | collective-permute-start | bytes 393224 | tf_op jit(solution)/shard_map/ppermute | solution.py:48
  916.9 15.0 %collective-permute-start.105 = (bf16[9,2,2,16,512]{4,3,2,1,0:T(8,128)(2,1)S(1)}, bf16[9,2,2,16,512]{4,3,2,1,0:T(8,128)(2,1)S(1)}, u32[]{:S(2)}, u32[]{:S(2)}) collective-permute-start(bf16[9,2,2,16,512]{4,3,2,1,0:T(8,128)(2,1)S(1)} %dynamic-slice_bitcast_fusion.6), channel_id=1, source_target_pairs={{0,4},{1,5},{2,6},{3,7},{4,0},{5,1},{6,2},{7,3},{8,12},{9,13},{10,... | collective-permute-start | bytes 1769480 | tf_op jit(solution)/shard_map/ppermute | solution.py:48
  (221 other events, 4009.0 us)
